TPU v7x, 512 devices: a whole 4x8x8 slice. The times are simulated.
512 devices in a mesh: grid: 64 (over x, z, core), band: 8 (over y).
Axes of the slice: x: 4, y: 8, z: 8, core: 2. Of those that a mesh axis runs over, the one named last changes fastest.
Arguments:
- orbitals: float32 [128, 256, 16, 128], P('band', 'grid'), may hold values from -16 to 16
- potential: float32 [256, 16, 128], P('grid'), may hold values from 0 to 2
Outputs:
- filtered: float32 [128, 256, 16, 128], P('band', 'grid')
- intersection: float32 [128, 128], P('band')
- hamiltonian: float32 [128, 128], P('band')
All inputs are finite; a program needn't handle non-finite values.
Results may differ from a plain program's by a relative error of at most 0.00011.
Values sent between devices are 32-bit elements; how exact they have to be, the bound alone decides.
No kernel may reach another device: no remote copies, remote signals or barrier semaphores. Data moves between devices by JAX's collectives and lax.ppermute only.
A program may use at most 64 MiB of HBM per device.

v0:
```python
import jax
import jax.numpy as jnp
from jax import lax
from jax.sharding import PartitionSpec as P

SHIFT_MID = 6.5
HALF_WIDTH = 3.5


def padded_2(block, sides, width):
    for axis, dim in sides:
        count = lax.axis_size(axis)
        forward = [(i, i + 1) for i in range(count - 1)]
        forward.append((count - 1, 0))
        backward = [(target, source) for source, target in forward]
        low = lax.ppermute(
            lax.slice_in_dim(block, block.shape[dim] - width, None, axis=dim), axis, forward
        )
        high = lax.ppermute(lax.slice_in_dim(block, 0, width, axis=dim), axis, backward)
        block = jnp.concatenate([low, block, high], axis=dim)
    return block


def stencil_roll(field, axis_id):
    return (
        -jnp.roll(field, 2, axis_id)
        + 16.0 * jnp.roll(field, 1, axis_id)
        - 30.0 * field
        + 16.0 * jnp.roll(field, -1, axis_id)
        - jnp.roll(field, -2, axis_id)
    ) / 12.0


def stencil_padded(padded):
    return (
        -padded[:, :-4]
        + 16.0 * padded[:, 1:-3]
        - 30.0 * padded[:, 2:-2]
        + 16.0 * padded[:, 3:-1]
        - padded[:, 4:]
    ) / 12.0


def apply_op(padded, pot_inner):
    center = padded[:, 2:-2]
    laplacian = stencil_padded(padded) + stencil_roll(center, 2) + stencil_roll(center, 3)
    return -0.5 * laplacian + pot_inner[None] * center


def with_planes(field, pot_own):
    padded = padded_2(field, (("grid", 1),), 2)
    return apply_op(padded, pot_own)


def per_device(orbitals, potential):
    prior = orbitals
    current = (with_planes(orbitals, potential) - SHIFT_MID * orbitals) / HALF_WIDTH
    for repeat in range(3):
        following = (
            2.0 * (with_planes(current, potential) - SHIFT_MID * current) / HALF_WIDTH - prior
        )
        prior, current = (current, following)
    image = with_planes(current, potential)
    local_orbs = current.shape[0]
    cells_all = current.shape[1] * lax.axis_size("grid") * current.shape[2] * current.shape[3]
    own_flat = current.reshape(local_orbs, -1)
    own_image = image.reshape(local_orbs, -1)
    piece = lax.all_gather(current, "band", axis=0, tiled=True)
    others = piece.reshape(piece.shape[0], -1)
    over_rows = jnp.dot(
        own_flat, others.T, precision=lax.Precision.HIGHEST, preferred_element_type=jnp.float32
    )
    ham_rows = jnp.dot(
        own_image, others.T, precision=lax.Precision.HIGHEST, preferred_element_type=jnp.float32
    )
    rows_both = jnp.stack([over_rows, ham_rows])
    totals = lax.psum(rows_both, "grid")
    intersection = totals[0] / cells_all
    hamiltonian = totals[1] / cells_all
    return (current, intersection, hamiltonian)


def solution(mesh):
    in_specs = (P("band", "grid", None, None), P("grid", None, None))
    out_specs = (P("band", "grid", None, None), P("band", None), P("band", None))
    return jax.shard_map(
        per_device, mesh=mesh, in_specs=in_specs, out_specs=out_specs, check_vma=False
    )
```

profile of v0, /device:TPU:1, one launch (start us, length us, event | category | flops | bytes accessed | tf_op | source)
XLA Modules:
  0.0 398.0 jit_solution(8345838602622504481)
XLA Ops:
  7.2 1.1 fusion.181
  8.5 5.4 %collective-permute-start = (f32[16,2,16,128]{3,0,2,1:T(8,128)S(1)}, f32[16,2,16,128]{3,0,2,1:T(8,128)S(1)}, u32[]{:S(2)}, u32[]{:S(2)}) collective-permute-start(f32[16,2,16,128]{3,0,2,1:T(8,128)S(1)} %copy.37), channel_id=1, source_target_pairs={{0,8},{8,16},{16,24},{24,32},{32,40},{40,48},{48,56},{56,64},{64,7... | collective-permute-start | bytes 786440 | tf_op jit(solution)/shard_map/ppermute | solution.py:16
  14.1 5.3 %collective-permute-start.1 = (f32[16,2,16,128]{3,0,2,1:T(8,128)S(1)}, f32[16,2,16,128]{3,0,2,1:T(8,128)S(1)}, u32[]{:S(2)}, u32[]{:S(2)}) collective-permute-start(f32[16,2,16,128]{3,0,2,1:T(8,128)S(1)} %copy.36), channel_id=1, source_target_pairs={{8,0},{16,8},{24,16},{32,24},{40,32},{48,40},{56,48},{64,56},{72,6... | collective-permute-start | bytes 786440 | tf_op jit(solution)/shard_map/ppermute | solution.py:19
  19.4 1.4 fusion.187
  25.9 1.2 broadcast_multiply_fusion
  28.0 1.9 collective-permute-start.2
  30.0 7.2 %collective-permute-start.3 = (f32[16,2,16,128]{3,0,2,1:T(8,128)S(1)}, f32[16,2,16,128]{3,0,2,1:T(8,128)S(1)}, u32[]{:S(2)}, u32[]{:S(2)}) collective-permute-start(f32[16,2,16,128]{3,0,2,1:T(8,128)S(1)} %get-tuple-element.79), channel_id=1, source_target_pairs={{8,0},{16,8},{24,16},{32,24},{40,32},{48,40},{56,48},{64,56},{72,6... | collective-permute-start | bytes 786440 | tf_op jit(solution)/shard_map/ppermute | solution.py:19
  37.3 1.0 collective-permute-done.3
  38.3 1.2 fusion.54
  40.5 1.9 collective-permute-start.4
  42.5 9.7 %collective-permute-start.5 = (f32[16,2,16,128]{3,0,2,1:T(8,128)S(1)}, f32[16,2,16,128]{3,0,2,1:T(8,128)S(1)}, u32[]{:S(2)}, u32[]{:S(2)}) collective-permute-start(f32[16,2,16,128]{3,0,2,1:T(8,128)S(1)} %get-tuple-element.61), channel_id=1, source_target_pairs={{8,0},{16,8},{24,16},{32,24},{40,32},{48,40},{56,48},{64,56},{72,6... | collective-permute-start | bytes 786440 | tf_op jit(solution)/shard_map/ppermute | solution.py:19
  52.3 1.0 collective-permute-done.5
  53.3 0.9 fusion.39
  55.2 1.9 collective-permute-start.6
  57.1 10.0 %collective-permute-start.7 = (f32[16,2,16,128]{3,0,2,1:T(8,128)S(1)}, f32[16,2,16,128]{3,0,2,1:T(8,128)S(1)}, u32[]{:S(2)}, u32[]{:S(2)}) collective-permute-start(f32[16,2,16,128]{3,0,2,1:T(8,128)S(1)} %get-tuple-element.43), channel_id=1, source_target_pairs={{8,0},{16,8},{24,16},{32,24},{40,32},{48,40},{56,48},{64,56},{72,6... | collective-permute-start | bytes 786440 | tf_op jit(solution)/shard_map/ppermute | solution.py:19
  67.3 0.9 collective-permute-done.7
  68.1 1.7 fusion.24
  69.9 2.1 copy.29
  71.9 1.9 fusion.153
  73.8 1.9 collective-permute-start.8
  75.7 9.9 %collective-permute-start.9 = (f32[16,2,16,128]{3,0,2,1:T(8,128)}, f32[16,2,16,128]{3,0,2,1:T(8,128)}, u32[]{:S(2)}, u32[]{:S(2)}) collective-permute-start(f32[16,2,16,128]{3,0,2,1:T(8,128)} %get-tuple-element.25), channel_id=1, source_target_pairs={{8,0},{16,8},{24,16},{32,24},{40,32},{48,40},{56,48},{64,56},{72,6... | collective-permute-start | bytes 786440 | tf_op jit(solution)/shard_map/ppermute | solution.py:19
  85.6 0.8 fusion.152
  86.4 0.9 fusion.150
  87.3 2.2 fusion.149
  89.5 1.0 fusion.151
  90.9 1.0 fusion.148
  91.9 1.1 fusion.145
  93.1 39.8 %all-gather.2.cloned.1.call-done = f32[128,4,16,128]{3,0,2,1:T(8,128)} async-done(((f32[16,4,16,128]{3,0,2,1:T(8,128)}), f32[128,4,16,128]{3,0,2,1:T(8,128)}) %all-gather.2.cloned.1.call-update) | async-done | bytes 4194320 | tf_op jit(solution)/shard_map/all_gather | solution.py:68
  132.9 5.3 %convolution_bitcast_fusion.1 = f32[1,16,128]{2,1,0:T(8,128)S(1)} fusion(f32[16,4,16,128]{3,0,2,1:T(8,128)S(1)} %copy-done, f32[128,4,16,128]{3,0,2,1:T(8,128)} %all-gather.2.cloned.1.call-done), kind=kOutput, calls=%fused_computation.1 | convolution fusion | flops 201326592 | bytes 4726784 | tf_op jit(solution)/shard_map/dot_general | solution.py:70
  138.2 5.7 %convolution_bitcast_fusion = f32[1,16,128]{2,1,0:T(8,128)S(1)} fusion(f32[128,4,16,128]{3,0,2,1:T(8,128)S(1)} %copy-done.2, f32[16,4,16,128]{3,0,2,1:T(8,128)S(1)} %copy-done, f32[16,2,16,128]{3,0,2,1:T(8,128)} %collective-permute-done.9, f32[16,2,16,128]{3,0,2,1:T(8,128)} %collective-permute-done.8, f32[16,4,14,128]{3,0,2,1:T(8,128)} %get-tuple-element.17, ...), kind=kOutput, calls=%fused_computation | convolution fusion | flops 206438400 | bytes 9478144 | tf_op jit(solution)/shard_map/dot_general | solution.py:73
  143.9 246.6 %psum.7 = f32[2,16,128]{2,1,0:T(8,128)S(1)} all-reduce(f32[2,16,128]{2,1,0:T(8,128)S(1)} %pad_maximum_fusion.9), channel_id=1, replica_groups=mesh['grid'=64,'band'=8] {'grid'}, use_global_device_ids=true, to_apply=%region_0.1 | all-reduce | flops 4096 | bytes 32768 | tf_op jit(solution)/shard_map/psum | solution.py:77
  390.6 0.6 fusion.138
  (78 shorter events, 8.8 us)
Async XLA Ops:
  7.2 13.7 %copy-start.1 = (f32[16,4,16,128]{3,2,1,0:T(8,128)S(1)}, f32[16,4,16,128]{3,2,1,0:T(8,128)}, u32[]{:S(2)}) copy-start(f32[16,4,16,128]{3,2,1,0:T(8,128)} %param.2) | copy-start | bytes 1572868
  7.2 125.7 %all-gather.2.cloned.1.call-start = ((), (), s32[]{:S(2)}) async-start(), calls=%async_computation | async-start | bytes 4718592 | tf_op jit(solution)/shard_map/all_gather | solution.py:68
  8.5 17.0 %collective-permute-start = (f32[16,2,16,128]{3,0,2,1:T(8,128)S(1)}, f32[16,2,16,128]{3,0,2,1:T(8,128)S(1)}, u32[]{:S(2)}, u32[]{:S(2)}) collective-permute-start(f32[16,2,16,128]{3,0,2,1:T(8,128)S(1)} %copy.37), channel_id=1, source_target_pairs={{0,8},{8,16},{16,24},{24,32},{32,40},{40,48},{48,56},{56,64},{64,7... | collective-permute-start | bytes 786440 | tf_op jit(solution)/shard_map/ppermute | solution.py:16
  14.1 11.8 %collective-permute-start.1 = (f32[16,2,16,128]{3,0,2,1:T(8,128)S(1)}, f32[16,2,16,128]{3,0,2,1:T(8,128)S(1)}, u32[]{:S(2)}, u32[]{:S(2)}) collective-permute-start(f32[16,2,16,128]{3,0,2,1:T(8,128)S(1)} %copy.36), channel_id=1, source_target_pairs={{8,0},{16,8},{24,16},{32,24},{40,32},{48,40},{56,48},{64,56},{72,6... | collective-permute-start | bytes 786440 | tf_op jit(solution)/shard_map/ppermute | solution.py:19
  23.0 2.5 copy-start.4
  28.0 9.2 %collective-permute-start.2 = (f32[16,2,16,128]{3,0,2,1:T(8,128)S(1)}, f32[16,2,16,128]{3,0,2,1:T(8,128)S(1)}, u32[]{:S(2)}, u32[]{:S(2)}) collective-permute-start(f32[16,2,16,128]{3,0,2,1:T(8,128)S(1)} %get-tuple-element.78), channel_id=1, source_target_pairs={{0,8},{8,16},{16,24},{24,32},{32,40},{40,48},{48,56},{56,64},{64,7... | collective-permute-start | bytes 786440 | tf_op jit(solution)/shard_map/ppermute | solution.py:16
  30.0 8.4 %collective-permute-start.3 = (f32[16,2,16,128]{3,0,2,1:T(8,128)S(1)}, f32[16,2,16,128]{3,0,2,1:T(8,128)S(1)}, u32[]{:S(2)}, u32[]{:S(2)}) collective-permute-start(f32[16,2,16,128]{3,0,2,1:T(8,128)S(1)} %get-tuple-element.79), channel_id=1, source_target_pairs={{8,0},{16,8},{24,16},{32,24},{40,32},{48,40},{56,48},{64,56},{72,6... | collective-permute-start | bytes 786440 | tf_op jit(solution)/shard_map/ppermute | solution.py:19
  40.5 11.7 %collective-permute-start.4 = (f32[16,2,16,128]{3,0,2,1:T(8,128)S(1)}, f32[16,2,16,128]{3,0,2,1:T(8,128)S(1)}, u32[]{:S(2)}, u32[]{:S(2)}) collective-permute-start(f32[16,2,16,128]{3,0,2,1:T(8,128)S(1)} %get-tuple-element.60), channel_id=1, source_target_pairs={{0,8},{8,16},{16,24},{24,32},{32,40},{40,48},{48,56},{56,64},{64,7... | collective-permute-start | bytes 786440 | tf_op jit(solution)/shard_map/ppermute | solution.py:16
  42.5 10.8 %collective-permute-start.5 = (f32[16,2,16,128]{3,0,2,1:T(8,128)S(1)}, f32[16,2,16,128]{3,0,2,1:T(8,128)S(1)}, u32[]{:S(2)}, u32[]{:S(2)}) collective-permute-start(f32[16,2,16,128]{3,0,2,1:T(8,128)S(1)} %get-tuple-element.61), channel_id=1, source_target_pairs={{8,0},{16,8},{24,16},{32,24},{40,32},{48,40},{56,48},{64,56},{72,6... | collective-permute-start | bytes 786440 | tf_op jit(solution)/shard_map/ppermute | solution.py:19
  55.2 12.1 %collective-permute-start.6 = (f32[16,2,16,128]{3,0,2,1:T(8,128)S(1)}, f32[16,2,16,128]{3,0,2,1:T(8,128)S(1)}, u32[]{:S(2)}, u32[]{:S(2)}) collective-permute-start(f32[16,2,16,128]{3,0,2,1:T(8,128)S(1)} %get-tuple-element.42), channel_id=1, source_target_pairs={{0,8},{8,16},{16,24},{24,32},{32,40},{40,48},{48,56},{56,64},{64,7... | collective-permute-start | bytes 786440 | tf_op jit(solution)/shard_map/ppermute | solution.py:16
  57.1 11.0 %collective-permute-start.7 = (f32[16,2,16,128]{3,0,2,1:T(8,128)S(1)}, f32[16,2,16,128]{3,0,2,1:T(8,128)S(1)}, u32[]{:S(2)}, u32[]{:S(2)}) collective-permute-start(f32[16,2,16,128]{3,0,2,1:T(8,128)S(1)} %get-tuple-element.43), channel_id=1, source_target_pairs={{8,0},{16,8},{24,16},{32,24},{40,32},{48,40},{56,48},{64,56},{72,6... | collective-permute-start | bytes 786440 | tf_op jit(solution)/shard_map/ppermute | solution.py:19
  69.8 19.6 %copy-start = (f32[16,4,16,128]{3,0,2,1:T(8,128)S(1)}, f32[16,4,16,128]{3,0,2,1:T(8,128)}, u32[]{:S(2)}) copy-start(f32[16,4,16,128]{3,0,2,1:T(8,128)} %fusion.24) | copy-start | bytes 1572868
  73.8 64.4 %collective-permute-start.8 = (f32[16,2,16,128]{3,0,2,1:T(8,128)}, f32[16,2,16,128]{3,0,2,1:T(8,128)}, u32[]{:S(2)}, u32[]{:S(2)}) collective-permute-start(f32[16,2,16,128]{3,0,2,1:T(8,128)} %get-tuple-element.24), channel_id=1, source_target_pairs={{0,8},{8,16},{16,24},{24,32},{32,40},{40,48},{48,56},{56,64},{64,7... | collective-permute-start | bytes 786440 | tf_op jit(solution)/shard_map/ppermute | solution.py:16
  75.7 62.5 %collective-permute-start.9 = (f32[16,2,16,128]{3,0,2,1:T(8,128)}, f32[16,2,16,128]{3,0,2,1:T(8,128)}, u32[]{:S(2)}, u32[]{:S(2)}) collective-permute-start(f32[16,2,16,128]{3,0,2,1:T(8,128)} %get-tuple-element.25), channel_id=1, source_target_pairs={{8,0},{16,8},{24,16},{32,24},{40,32},{48,40},{56,48},{64,56},{72,6... | collective-permute-start | bytes 786440 | tf_op jit(solution)/shard_map/ppermute | solution.py:19
  132.9 5.3 %copy-start.2 = (f32[128,4,16,128]{3,0,2,1:T(8,128)S(1)}, f32[128,4,16,128]{3,0,2,1:T(8,128)}, u32[]{:S(2)}) copy-start(f32[128,4,16,128]{3,0,2,1:T(8,128)} %all-gather.2.cloned.1.call-done) | copy-start | bytes 12582916
  132.9 5.3 %copy-start.3 = (f32[16,4,16,1]{3,0,2,1:T(8,128)S(1)}, f32[16,4,16,1]{3,0,2,1:T(8,128)}, u32[]{:S(2)}) copy-start(f32[16,4,16,1]{3,0,2,1:T(8,128)} %get-tuple-element.15) | copy-start | bytes 12292
Sparse Core Ops, SparseCore 0:
  70.0 62.8 all-gather.1
where the time goes:
time: 402 us; the launch traced here: 398 us
  blocking collectives  247 us (61%)
  starting transfers between devices  55.2 us (14%)
  waiting for transfers between devices  42.8 us (11%)
  local copies, waits for them, and re-layouts  22.2 us (6%)
  between operations  14.5 us (4%)
  matrix products  11 us (3%)
  other arithmetic  5.67 us (1%)
    psum x1, blocking collectives, per_device(): totals = lax.psum(rows_both, 'grid')  247 us
    ppermute x5, starting transfers between devices, padded_2(): lax.ppermute(lax.slice_in_dim(block, 0, width, axis=dim), axis, backward)  42.1 us
    all_gather x1, waiting for transfers between devices, per_device(): piece = lax.all_gather(current, 'band', axis=0, tiled=True)  39.8 us
    ppermute x5, starting transfers between devices, padded_2(): lax.ppermute(lax.slice_in_dim(block, block.shape[dim] - width, None, axis...  13.1 us
  transfers between devices with their start and end apart: 11, of which 4 were waited for; matrix products, arithmetic and copies ran while one was open for 6% of the time, Pallas kernels for 0%

commit v1 on v0

v1 whole, which is shorter than its diff:
```python
import jax
import jax.numpy as jnp
from jax import lax
from jax.experimental import pallas as pl
from jax.experimental.pallas import tpu as pltpu
from jax.sharding import Mesh, PartitionSpec as P

SHIFT_MID = 6.5
HALF_WIDTH = 3.5
DIAG = 3.0 * 30.0 / 24.0
NEAR = -16.0 / 24.0
FAR = 1.0 / 24.0
GRID = ("x", "z", "core")
VMEM = pl.BlockSpec(memory_space=pltpu.VMEM)
LIMIT = pltpu.CompilerParams(vmem_limit_bytes=24 * 1024 * 1024)


def ring_shift(size, by):
    return [(i, (i + by) % size) for i in range(size)]


def scaled_op(padded, diag):
    mid = padded[2:-2]
    rows, lanes = mid.shape[1], mid.shape[2]
    near = padded[1:-3] + padded[3:-1]
    far = padded[:-4] + padded[4:]
    near = near + (pltpu.roll(mid, 1, 1) + pltpu.roll(mid, rows - 1, 1))
    far = far + (pltpu.roll(mid, 2, 1) + pltpu.roll(mid, rows - 2, 1))
    near = near + (pltpu.roll(mid, 1, 2) + pltpu.roll(mid, lanes - 1, 2))
    far = far + (pltpu.roll(mid, 2, 2) + pltpu.roll(mid, lanes - 2, 2))
    return diag * mid + (NEAR / HALF_WIDTH) * near + (FAR / HALF_WIDTH) * far


def scaled_diag(vlo, vown, vhi):
    v = jnp.concatenate([vlo[...], vown[...], vhi[...]], axis=0)
    return (v + (DIAG - SHIFT_MID)) / HALF_WIDTH


def stage_one(flo, fown, fhi, vlo, vown, vhi, out):
    diag = scaled_diag(vlo, vown, vhi)

    def step(o, carry):
        f = jnp.concatenate([flo[o], fown[o], fhi[o]], axis=0)
        first = scaled_op(f, diag)
        out[o] = 2.0 * scaled_op(first, diag[2:-2]) - fown[o]
        return carry

    lax.fori_loop(0, fown.shape[0], step, 0)


def stage_two(glo, gown, ghi, fown, vlo, vown, vhi, out, edge):
    diag = scaled_diag(vlo, vown, vhi)

    def step(o, carry):
        g = jnp.concatenate([glo[o], gown[o], ghi[o]], axis=0)
        first = scaled_op(g, diag)
        u = 4.0 * scaled_op(first, diag[2:-2]) - 2.0 * gown[o] - fown[o]
        out[o] = u
        edge[o] = u[:2]
        return carry

    lax.fori_loop(0, fown.shape[0], step, 0)


def stage_half(uown, unext, vown, out):
    orbs, planes, rows, lanes = uown.shape
    half_diag = 0.5 * (vown[...] + DIAG)

    def step(o, carry):
        u = uown[o]
        up = jnp.concatenate([u, unext[o]], axis=0)
        near = up[1:-1] + pltpu.roll(u, rows - 1, 1) + pltpu.roll(u, lanes - 1, 2)
        far = up[2:] + pltpu.roll(u, rows - 2, 1) + pltpu.roll(u, lanes - 2, 2)
        w = half_diag * u + NEAR * near + FAR * far
        for plane in range(planes):
            for part in range(rows // 8):
                peer = plane * (rows // 8) + part
                out[peer, 0, :, pl.ds(o, 1), :] = u[plane, part * 8 : part * 8 + 8][:, None, :]
                out[peer, 1, :, pl.ds(o, 1), :] = w[plane, part * 8 : part * 8 + 8][:, None, :]
        return carry

    lax.fori_loop(0, orbs, step, 0)


def gram(blocks, out):
    bands, _, rows, orbs, lanes = blocks.shape
    total = bands * orbs
    dims = (((1,), (1,)), ((), ()))

    def dot(a, b):
        return lax.dot_general(a, b, dims, precision=lax.Precision.HIGHEST, preferred_element_type=jnp.float32)

    over = jnp.zeros((total, total), jnp.float32)
    half = jnp.zeros((total, total), jnp.float32)
    for row in range(rows):
        f = blocks[:, 0, row].reshape(total, lanes)
        w = blocks[:, 1, row].reshape(total, lanes)
        over = over + dot(f, f)
        half = half + dot(f, w)
    ham = half + half.T
    out[:, 0] = over.reshape(bands, orbs, total)
    out[:, 1] = ham.reshape(bands, orbs, total)


def call(body, out_shapes, *args):
    return pl.pallas_call(
        body,
        out_shape=[jax.ShapeDtypeStruct(s, jnp.float32) for s in out_shapes],
        in_specs=[VMEM] * len(args),
        out_specs=[VMEM] * len(out_shapes),
        compiler_params=LIMIT,
    )(*args)


def per_device(orbitals, potential):
    orbs, planes, rows, lanes = orbitals.shape
    slabs = lax.axis_size(GRID)
    bands = lax.axis_size("y")
    cells_all = slabs * planes * rows * lanes
    up, down = ring_shift(slabs, 1), ring_shift(slabs, -1)

    flo = lax.ppermute(orbitals, GRID, up)
    fhi = lax.ppermute(orbitals, GRID, down)
    vlo = lax.ppermute(potential[planes - 2 :], GRID, up)
    vhi = lax.ppermute(potential[:2], GRID, down)
    (g,) = call(stage_one, [orbitals.shape], flo, orbitals, fhi, vlo, potential, vhi)

    glo = lax.ppermute(g, GRID, up)
    ghi = lax.ppermute(g, GRID, down)
    u, edge = call(
        stage_two, [orbitals.shape, (orbs, 2, rows, lanes)], glo, g, ghi, orbitals, vlo, potential, vhi
    )

    unext = lax.ppermute(edge, GRID, down)
    (send,) = call(stage_half, [(bands, 2, planes * rows // bands, orbs, lanes)], u, unext, potential)
    got = lax.all_to_all(send, "y", 0, 0, tiled=True)
    (part,) = call(gram, [(bands, 2, orbs, bands * orbs)], got)

    first = ("y", "x", "core")
    pieces = lax.axis_size(first)
    flat = part.reshape(pieces, -1, bands * orbs)
    mine = lax.all_to_all(flat, first, 0, 0, tiled=True).sum(0)
    spread = jnp.broadcast_to(mine[None], (slabs, *mine.shape))
    back = lax.all_to_all(spread, GRID, 0, 0, tiled=True)
    nx, nz, nc = (lax.axis_size(a) for a in GRID)
    both = back.reshape(nx, nz, nc, *mine.shape).sum(1) / cells_all
    both = both.reshape(2, orbs, bands * orbs)
    return u, both[0], both[1]


def solution(mesh):
    devices = mesh.devices.reshape(4, 8, 2, 8)
    fine = Mesh(devices, ("x", "z", "core", "y"))
    in_specs = (P("y", GRID, None, None), P(GRID, None, None))
    out_specs = (P("y", GRID, None, None), P("y", None), P("y", None))
    return jax.shard_map(per_device, mesh=fine, in_specs=in_specs, out_specs=out_specs, check_vma=False)
```

time: 402 us -> 132 us (0.33)
  blocking collectives: 247 us -> 65 us
  waiting for transfers between devices: 42.8 us -> 12.9 us
  local copies, waits for them, and re-layouts: 22.2 us -> 3.45 us
  starting transfers between devices: 55.2 us -> 37.2 us
  between operations: 14.5 us -> 0.76 us
  Pallas kernels: 0 us -> 11.8 us
  matrix products: 11 us -> 0 us
  other arithmetic: 5.67 us -> 0.11 us
    psum x1 -> x0, blocking collectives: 247 us -> none  [per_device(): totals = lax.psum(rows_both, 'grid')]
    all_to_all x0 -> x3, blocking collectives: none -> 65 us  [the longest x1 31.6 us: per_device(): got = lax.all_to_all(send, 'y', 0, 0, tiled=True)]
    all_gather x1 -> x0, waiting for transfers between devices: 39.8 us -> none  [per_device(): piece = lax.all_gather(current, 'band', axis=0, tiled=True)]
    ppermute x10 -> x7, starting transfers between devices: 55.2 us -> 37.2 us  [the longest x1 8.79 us: per_device(): fhi = lax.ppermute(orbitals, GRID, down)]
    slice x45 -> x2, local copies, waits for them, and re-layouts: 15.8 us -> 1.34 us  [the longest x1 0.74 us: per_device(): vhi = lax.ppermute(potential[:2], GRID, down)]
    pallas_call x0 -> x4, Pallas kernels: none -> 11.8 us  [call(): pl.pallas_call(body, out_shape=[jax.ShapeDtypeStruct(s, jnp.float32) for...]
    dot_general x2 -> x0, matrix products: 11 us -> none  [the longest x1 5.71 us: per_device(): jnp.dot(own_image, others.T, precision=lax.Precision.HIGHEST, preferred_e...]
    ppermute x10 -> x7, waiting for transfers between devices: 2.94 us -> 12.9 us  [the longest x1 5.69 us: per_device(): vlo = lax.ppermute(potential[planes - 2:], GRID, up)]
  transfers between devices with their start and end apart: 11 -> 7, of which waited for: 4 -> 4; matrix products, arithmetic and copies ran while one was open for 6% -> 1% of each run, Pallas kernels for 0% -> 0%
where the time goes in v1:
time: 132 us; the launch traced here: 131 us
  blocking collectives  65 us (49%)
  starting transfers between devices  37.2 us (28%)
  waiting for transfers between devices  12.9 us (10%)
  Pallas kernels  11.8 us (9%)
  local copies, waits for them, and re-layouts  3.45 us (3%)
    all_to_all x1, blocking collectives, per_device(): got = lax.all_to_all(send, 'y', 0, 0, tiled=True)  31.6 us
    all_to_all x1, blocking collectives, per_device(): mine = lax.all_to_all(flat, first, 0, 0, tiled=True).sum(0)  19.3 us
    all_to_all x1, blocking collectives, per_device(): back = lax.all_to_all(spread, GRID, 0, 0, tiled=True)  14.1 us
    pallas_call x4, Pallas kernels, call(): pl.pallas_call(body, out_shape=[jax.ShapeDtypeStruct(s, jnp.float32) for...  11.8 us
    ppermute x1, starting transfers between devices, per_device(): fhi = lax.ppermute(orbitals, GRID, down)  8.79 us
    ppermute x1, starting transfers between devices, per_device(): ghi = lax.ppermute(g, GRID, down)  7.71 us
    ppermute x1, starting transfers between devices, per_device(): unext = lax.ppermute(edge, GRID, down)  7.7 us
    ppermute x1, starting transfers between devices, per_device(): vhi = lax.ppermute(potential[:2], GRID, down)  7.2 us
  transfers between devices with their start and end apart: 7, of which 4 were waited for; matrix products, arithmetic and copies ran while one was open for 1% of the time, Pallas kernels for 0%

profile of v1, /device:TPU:1, one launch (start us, length us, event | category | flops | bytes accessed | tf_op | source)
XLA Modules:
  0.0 131.2 jit_solution(13448569758529396732)
XLA Ops:
  0.6 0.0 copy-start.2
  0.6 8.8 %collective-permute-start.1 = (f32[16,4,16,128]{3,2,1,0:T(8,128)}, f32[16,4,16,128]{3,2,1,0:T(8,128)S(1)}, u32[]{:S(2)}, u32[]{:S(2)}) collective-permute-start(f32[16,4,16,128]{3,2,1,0:T(8,128)} %fown.3), channel_id=1, source_target_pairs={{0,504},{8,0},{16,8},{24,16},{32,24},{40,32},{48,40},{56,48},{64,5... | collective-permute-start | bytes 1572872 | tf_op jit(solution)/shard_map/ppermute | solution.py:123
  9.4 1.9 %collective-permute-start = (f32[16,4,16,128]{3,2,1,0:T(8,128)}, f32[16,4,16,128]{3,2,1,0:T(8,128)S(1)}, u32[]{:S(2)}, u32[]{:S(2)}) collective-permute-start(f32[16,4,16,128]{3,2,1,0:T(8,128)} %fown.3), channel_id=1, source_target_pairs={{0,8},{8,16},{16,24},{24,32},{32,40},{40,48},{48,56},{56,64},{64,7... | collective-permute-start | bytes 1572872 | tf_op jit(solution)/shard_map/ppermute | solution.py:122
  11.4 0.7 fusion
  12.1 7.2 %collective-permute-start.3 = (f32[2,16,128]{2,1,0:T(8,128)S(1)}, f32[2,16,128]{2,1,0:T(8,128)S(1)}, u32[]{:S(2)}, u32[]{:S(2)}) collective-permute-start(f32[2,16,128]{2,1,0:T(8,128)S(1)} %get-tuple-element.7), channel_id=1, source_target_pairs={{0,504},{8,0},{16,8},{24,16},{32,24},{40,32},{48,40},{56,48},{64,5... | collective-permute-start | bytes 49160 | tf_op jit(solution)/shard_map/ppermute | solution.py:125
  19.3 1.9 %collective-permute-start.2 = (f32[2,16,128]{2,1,0:T(8,128)S(1)}, f32[2,16,128]{2,1,0:T(8,128)S(1)}, u32[]{:S(2)}, u32[]{:S(2)}) collective-permute-start(f32[2,16,128]{2,1,0:T(8,128)S(1)} %get-tuple-element.8), channel_id=1, source_target_pairs={{0,8},{8,16},{16,24},{24,32},{32,40},{40,48},{48,56},{56,64},{64,7... | collective-permute-start | bytes 49160 | tf_op jit(solution)/shard_map/ppermute | solution.py:124
  21.2 0.0 collective-permute-done.3.vhi
  21.2 5.7 %collective-permute-done.2.vlo = f32[2,16,128]{2,1,0:T(8,128)S(1)} collective-permute-done((f32[2,16,128]{2,1,0:T(8,128)S(1)}, f32[2,16,128]{2,1,0:T(8,128)S(1)}, u32[]{:S(2)}, u32[]{:S(2)}) %collective-permute-start.2) | collective-permute-done | bytes 16416 | tf_op jit(solution)/shard_map/ppermute | solution.py:124
  26.9 0.0 collective-permute-done.1.fhi
  26.9 0.0 collective-permute-done.flo
  27.0 0.0 copy-done.2
  27.0 0.0 copy-start
  27.0 1.0 copy-done
  28.0 0.0 copy-start.1
  28.0 3.5 %shard_map.49.gown = f32[16,4,16,128]{3,2,1,0:T(8,128)S(1)} custom-call(f32[16,4,16,128]{3,2,1,0:T(8,128)S(1)} %collective-permute-done.flo, f32[16,4,16,128]{3,2,1,0:T(8,128)S(1)} %copy-done, f32[16,4,16,128]{3,2,1,0:T(8,128)S(1)} %collective-permute-done.1.fhi, f32[2,16,128]{2,1,0:T(8,128)S(1)} %collective-permute-done.2.vlo, f32[4,16,128]{2,1,0:T(8,128)S(1)} %copy-done.2, ...), custom_call_target="tpu_custom_call" | custom-call | tf_op jit(solution)/shard_map/pallas_call | solution.py:106
  31.5 7.7 %collective-permute-start.5 = (f32[16,4,16,128]{3,2,1,0:T(8,128)S(1)}, f32[16,4,16,128]{3,2,1,0:T(8,128)S(1)}, u32[]{:S(2)}, u32[]{:S(2)}) collective-permute-start(f32[16,4,16,128]{3,2,1,0:T(8,128)S(1)} %shard_map.49.gown), channel_id=1, source_target_pairs={{0,504},{8,0},{16,8},{24,16},{32,24},{40,32},{48,40},{56,48},{64,5... | collective-permute-start | bytes 1572872 | tf_op jit(solution)/shard_map/ppermute | solution.py:129
  39.2 1.9 %collective-permute-start.4 = (f32[16,4,16,128]{3,2,1,0:T(8,128)S(1)}, f32[16,4,16,128]{3,2,1,0:T(8,128)S(1)}, u32[]{:S(2)}, u32[]{:S(2)}) collective-permute-start(f32[16,4,16,128]{3,2,1,0:T(8,128)S(1)} %shard_map.49.gown), channel_id=1, source_target_pairs={{0,8},{8,16},{16,24},{24,32},{32,40},{40,48},{48,56},{56,64},{64,7... | collective-permute-start | bytes 1572872 | tf_op jit(solution)/shard_map/ppermute | solution.py:128
  41.1 0.9 collective-permute-done.5.ghi
  42.0 5.2 %collective-permute-done.4.glo = f32[16,4,16,128]{3,2,1,0:T(8,128)S(1)} collective-permute-done((f32[16,4,16,128]{3,2,1,0:T(8,128)S(1)}, f32[16,4,16,128]{3,2,1,0:T(8,128)S(1)}, u32[]{:S(2)}, u32[]{:S(2)}) %collective-permute-start.4) | collective-permute-done | bytes 524320 | tf_op jit(solution)/shard_map/ppermute | solution.py:128
  47.2 0.0 copy-done.1
  47.2 4.3 %shard_map.50 = (f32[16,4,16,128]{3,2,1,0:T(8,128)}, f32[16,2,16,128]{3,2,1,0:T(8,128)S(1)}) custom-call(f32[16,4,16,128]{3,2,1,0:T(8,128)S(1)} %collective-permute-done.4.glo, f32[16,4,16,128]{3,2,1,0:T(8,128)S(1)} %shard_map.49.gown, f32[16,4,16,128]{3,2,1,0:T(8,128)S(1)} %collective-permute-done.5.ghi, f32[16,4,16,128]{3,2,1,0:T(8,128)S(1)} %copy-done.1, ...), custom_call_target="tpu_custom_call" | custom-call | tf_op jit(solution)/shard_map/pallas_call | solution.py:106
  51.5 7.7 %collective-permute-start.6 = (f32[16,2,16,128]{3,2,1,0:T(8,128)S(1)}, f32[16,2,16,128]{3,2,1,0:T(8,128)S(1)}, u32[]{:S(2)}, u32[]{:S(2)}) collective-permute-start(f32[16,2,16,128]{3,2,1,0:T(8,128)S(1)} %get-tuple-element.6), channel_id=1, source_target_pairs={{0,504},{8,0},{16,8},{24,16},{32,24},{40,32},{48,40},{56,48},{64,5... | collective-permute-start | bytes 786440 | tf_op jit(solution)/shard_map/ppermute | solution.py:134
  59.2 1.1 collective-permute-done.6.unext
  60.4 0.0 copy-start.3
  60.4 1.0 copy-done.3
  61.4 1.7 %shard_map.51 = f32[8,2,8,16,128]{4,3,2,1,0:T(8,128)S(1)} custom-call(f32[16,4,16,128]{3,2,1,0:T(8,128)S(1)} %copy-done.3, f32[16,2,16,128]{3,2,1,0:T(8,128)S(1)} %collective-permute-done.6.unext, f32[4,16,128]{2,1,0:T(8,128)S(1)} %copy-done.2), custom_call_target="tpu_custom_call" | custom-call | tf_op jit(solution)/shard_map/pallas_call | solution.py:106
  63.1 31.6 %all_to_all.15.blocks = f32[8,2,8,16,128]{4,3,2,1,0:T(8,128)S(1)} all-to-all(f32[8,2,8,16,128]{4,3,2,1,0:T(8,128)S(1)} %shard_map.51), channel_id=1, replica_groups=mesh['x'=4,'z'=8,'core'=2,'y'=8] {'y'}, dimensions={0} | all-to-all | bytes 2097152 | tf_op jit(solution)/shard_map/all_to_all | solution.py:136
  94.7 2.3 %shard_map.52 = f32[8,2,16,128]{3,2,1,0:T(8,128)S(1)} custom-call(f32[8,2,8,16,128]{4,3,2,1,0:T(8,128)S(1)} %all_to_all.15.blocks), custom_call_target="tpu_custom_call" | custom-call | tf_op jit(solution)/shard_map/pallas_call | solution.py:106
  97.1 19.3 %all_to_all.16 = f32[64,4,128]{2,1,0:T(4,128)S(1)} all-to-all(f32[64,4,128]{2,1,0:T(4,128)S(1)} %bitcast.4), channel_id=1, replica_groups=mesh['x'=4,'z'=8,'core'=2,'y'=8] {'y','x','core'}, dimensions={0} | all-to-all | bytes 262144 | tf_op jit(solution)/shard_map/all_to_all | solution.py:142
  116.4 0.1 reduce_sum.18
  116.5 14.1 %all_to_all.17 = f32[64,4,128]{2,1,0:T(4,128)S(1)} all-to-all(f32[64,4,128]{2,1,0:T(4,128)S(1)} %broadcast_in_dim.2), channel_id=1, replica_groups=mesh['x'=4,'z'=8,'core'=2,'y'=8] {'x','z','core'}, dimensions={0} | all-to-all | bytes 262144 | tf_op jit(solution)/shard_map/all_to_all | solution.py:144
  130.6 0.6 fusion.1
  (3 shorter events, 0.1 us)
Async XLA Ops:
  0.6 26.3 %copy-start.2 = (f32[4,16,128]{2,1,0:T(8,128)S(1)}, f32[4,16,128]{2,1,0:T(8,128)}, u32[]{:S(2)}) copy-start(f32[4,16,128]{2,1,0:T(8,128)} %vown.5) | copy-start | bytes 98308
  0.6 26.3 %collective-permute-start.1 = (f32[16,4,16,128]{3,2,1,0:T(8,128)}, f32[16,4,16,128]{3,2,1,0:T(8,128)S(1)}, u32[]{:S(2)}, u32[]{:S(2)}) collective-permute-start(f32[16,4,16,128]{3,2,1,0:T(8,128)} %fown.3), channel_id=1, source_target_pairs={{0,504},{8,0},{16,8},{24,16},{32,24},{40,32},{48,40},{56,48},{64,5... | collective-permute-start | bytes 1572872 | tf_op jit(solution)/shard_map/ppermute | solution.py:123
  9.4 17.5 %collective-permute-start = (f32[16,4,16,128]{3,2,1,0:T(8,128)}, f32[16,4,16,128]{3,2,1,0:T(8,128)S(1)}, u32[]{:S(2)}, u32[]{:S(2)}) collective-permute-start(f32[16,4,16,128]{3,2,1,0:T(8,128)} %fown.3), channel_id=1, source_target_pairs={{0,8},{8,16},{16,24},{24,32},{32,40},{40,48},{48,56},{56,64},{64,7... | collective-permute-start | bytes 1572872 | tf_op jit(solution)/shard_map/ppermute | solution.py:122
  12.1 9.1 %collective-permute-start.3 = (f32[2,16,128]{2,1,0:T(8,128)S(1)}, f32[2,16,128]{2,1,0:T(8,128)S(1)}, u32[]{:S(2)}, u32[]{:S(2)}) collective-permute-start(f32[2,16,128]{2,1,0:T(8,128)S(1)} %get-tuple-element.7), channel_id=1, source_target_pairs={{0,504},{8,0},{16,8},{24,16},{32,24},{40,32},{48,40},{56,48},{64,5... | collective-permute-start | bytes 49160 | tf_op jit(solution)/shard_map/ppermute | solution.py:125
  19.3 7.6 %collective-permute-start.2 = (f32[2,16,128]{2,1,0:T(8,128)S(1)}, f32[2,16,128]{2,1,0:T(8,128)S(1)}, u32[]{:S(2)}, u32[]{:S(2)}) collective-permute-start(f32[2,16,128]{2,1,0:T(8,128)S(1)} %get-tuple-element.8), channel_id=1, source_target_pairs={{0,8},{8,16},{16,24},{24,32},{32,40},{40,48},{48,56},{56,64},{64,7... | collective-permute-start | bytes 49160 | tf_op jit(solution)/shard_map/ppermute | solution.py:124
  27.0 1.0 copy-start
  28.0 19.2 %copy-start.1 = (f32[16,4,16,128]{3,2,1,0:T(8,128)S(1)}, f32[16,4,16,128]{3,2,1,0:T(8,128)}, u32[]{:S(2)}) copy-start(f32[16,4,16,128]{3,2,1,0:T(8,128)} %fown.3) | copy-start | bytes 1572868
  31.5 10.5 %collective-permute-start.5 = (f32[16,4,16,128]{3,2,1,0:T(8,128)S(1)}, f32[16,4,16,128]{3,2,1,0:T(8,128)S(1)}, u32[]{:S(2)}, u32[]{:S(2)}) collective-permute-start(f32[16,4,16,128]{3,2,1,0:T(8,128)S(1)} %shard_map.49.gown), channel_id=1, source_target_pairs={{0,504},{8,0},{16,8},{24,16},{32,24},{40,32},{48,40},{56,48},{64,5... | collective-permute-start | bytes 1572872 | tf_op jit(solution)/shard_map/ppermute | solution.py:129
  39.2 8.0 %collective-permute-start.4 = (f32[16,4,16,128]{3,2,1,0:T(8,128)S(1)}, f32[16,4,16,128]{3,2,1,0:T(8,128)S(1)}, u32[]{:S(2)}, u32[]{:S(2)}) collective-permute-start(f32[16,4,16,128]{3,2,1,0:T(8,128)S(1)} %shard_map.49.gown), channel_id=1, source_target_pairs={{0,8},{8,16},{16,24},{24,32},{32,40},{40,48},{48,56},{56,64},{64,7... | collective-permute-start | bytes 1572872 | tf_op jit(solution)/shard_map/ppermute | solution.py:128
  51.5 8.8 %collective-permute-start.6 = (f32[16,2,16,128]{3,2,1,0:T(8,128)S(1)}, f32[16,2,16,128]{3,2,1,0:T(8,128)S(1)}, u32[]{:S(2)}, u32[]{:S(2)}) collective-permute-start(f32[16,2,16,128]{3,2,1,0:T(8,128)S(1)} %get-tuple-element.6), channel_id=1, source_target_pairs={{0,504},{8,0},{16,8},{24,16},{32,24},{40,32},{48,40},{56,48},{64,5... | collective-permute-start | bytes 786440 | tf_op jit(solution)/shard_map/ppermute | solution.py:134
  60.4 1.0 copy-start.3

commit v2 on v1

--- a/solution.py
+++ b/solution.py
@@ -31,40 +31,48 @@
     return diag * mid + (NEAR / HALF_WIDTH) * near + (FAR / HALF_WIDTH) * far
 
 
-def scaled_diag(vlo, vown, vhi):
-    v = jnp.concatenate([vlo[...], vown[...], vhi[...]], axis=0)
-    return (v + (DIAG - SHIFT_MID)) / HALF_WIDTH
+def by_core(run, on, off):
+    core = lax.axis_index("core")
+    pl.when(core == 0)(lambda: run(off, on))
+    pl.when(core == 1)(lambda: run(on, off))
 
 
-def stage_one(flo, fown, fhi, vlo, vown, vhi, out):
-    diag = scaled_diag(vlo, vown, vhi)
+def stage_one(own, on, off, out, diag):
+    orbs = own.shape[0] - 1
 
-    def step(o, carry):
-        f = jnp.concatenate([flo[o], fown[o], fhi[o]], axis=0)
-        first = scaled_op(f, diag)
-        out[o] = 2.0 * scaled_op(first, diag[2:-2]) - fown[o]
-        return carry
+    def run(lo, hi):
+        v = jnp.concatenate([lo[orbs, 2:], own[orbs], hi[orbs, :2]], axis=0)
+        diag[...] = (v + (DIAG - SHIFT_MID)) / HALF_WIDTH
 
-    lax.fori_loop(0, fown.shape[0], step, 0)
+        def step(o, carry):
+            f = jnp.concatenate([lo[o], own[o], hi[o]], axis=0)
+            first = scaled_op(f, diag[...])
+            out[o] = 2.0 * scaled_op(first, diag[2:-2]) - own[o]
+            return carry
+
+        lax.fori_loop(0, orbs, step, 0)
+
+    by_core(run, on, off)
 
 
-def stage_two(glo, gown, ghi, fown, vlo, vown, vhi, out, edge):
-    diag = scaled_diag(vlo, vown, vhi)
+def stage_two(gown, on, off, fown, diag, out, edge):
+    def run(lo, hi):
+        def step(o, carry):
+            g = jnp.concatenate([lo[o], gown[o], hi[o]], axis=0)
+            first = scaled_op(g, diag[...])
+            u = 4.0 * scaled_op(first, diag[2:-2]) - 2.0 * gown[o] - fown[o]
+            out[o] = u
+            edge[o] = u[:2]
+            return carry
 
-    def step(o, carry):
-        g = jnp.concatenate([glo[o], gown[o], ghi[o]], axis=0)
-        first = scaled_op(g, diag)
-        u = 4.0 * scaled_op(first, diag[2:-2]) - 2.0 * gown[o] - fown[o]
-        out[o] = u
-        edge[o] = u[:2]
-        return carry
+        lax.fori_loop(0, gown.shape[0], step, 0)
 
-    lax.fori_loop(0, fown.shape[0], step, 0)
+    by_core(run, on, off)
 
 
-def stage_half(uown, unext, vown, out):
+def stage_half(uown, unext, diag, out):
     orbs, planes, rows, lanes = uown.shape
-    half_diag = 0.5 * (vown[...] + DIAG)
+    half_diag = 0.5 * (HALF_WIDTH * diag[2:-2] + SHIFT_MID)
 
     def step(o, carry):
         u = uown[o]
@@ -117,22 +125,21 @@
     slabs = lax.axis_size(GRID)
     bands = lax.axis_size("y")
     cells_all = slabs * planes * rows * lanes
-    up, down = ring_shift(slabs, 1), ring_shift(slabs, -1)
+    down = ring_shift(slabs, -1)
+    outer = [(i, (i + (1 if i % 2 else -1)) % slabs) for i in range(slabs)]
 
-    flo = lax.ppermute(orbitals, GRID, up)
-    fhi = lax.ppermute(orbitals, GRID, down)
-    vlo = lax.ppermute(potential[planes - 2 :], GRID, up)
-    vhi = lax.ppermute(potential[:2], GRID, down)
-    (g,) = call(stage_one, [orbitals.shape], flo, orbitals, fhi, vlo, potential, vhi)
+    def both_sides(slab):
+        off = lax.ppermute(slab, GRID, outer)
+        return lax.ppermute(slab, "core", [(0, 1), (1, 0)]), off
 
-    glo = lax.ppermute(g, GRID, up)
-    ghi = lax.ppermute(g, GRID, down)
+    slab = jnp.concatenate([orbitals, potential[None]], axis=0)
+    g, diag = call(stage_one, [orbitals.shape, (planes + 4, rows, lanes)], slab, *both_sides(slab))
     u, edge = call(
-        stage_two, [orbitals.shape, (orbs, 2, rows, lanes)], glo, g, ghi, orbitals, vlo, potential, vhi
+        stage_two, [orbitals.shape, (orbs, 2, rows, lanes)], g, *both_sides(g), slab, diag
     )
 
     unext = lax.ppermute(edge, GRID, down)
-    (send,) = call(stage_half, [(bands, 2, planes * rows // bands, orbs, lanes)], u, unext, potential)
+    (send,) = call(stage_half, [(bands, 2, planes * rows // bands, orbs, lanes)], u, unext, diag)
     got = lax.all_to_all(send, "y", 0, 0, tiled=True)
     (part,) = call(gram, [(bands, 2, orbs, bands * orbs)], got)
 

time: 132 us -> 122 us (0.924)
  waiting for transfers between devices: 12.9 us -> 5.4 us
  starting transfers between devices: 37.2 us -> 33.9 us
  blocking collectives: 65 us -> 67.2 us
  local copies, waits for them, and re-layouts: 3.45 us -> 1.67 us
    ppermute x6 -> x4, waiting for transfers between devices: 11.8 us -> 3.06 us  [the longest x2 3.06 us: both_sides(): return (lax.ppermute(slab, 'core', [(0, 1), (1, 0)]), off)]
    all_to_all x1, blocking collectives: 19.3 us -> 22.9 us  [per_device(): mine = lax.all_to_all(flat, first, 0, 0, tiled=True).sum(0)]
    all_to_all x1, blocking collectives: 31.6 us -> 28 us  [per_device(): got = lax.all_to_all(send, 'y', 0, 0, tiled=True)]
    ppermute x1, starting transfers between devices: 7.7 us -> 5.33 us  [per_device(): unext = lax.ppermute(edge, GRID, down)]
    all_to_all x1, blocking collectives: 14.1 us -> 16.3 us  [per_device(): back = lax.all_to_all(spread, GRID, 0, 0, tiled=True)]
    ppermute x6 -> x4, starting transfers between devices: 29.5 us -> 28.6 us  [the longest x2 21.3 us: both_sides(): return (lax.ppermute(slab, 'core', [(0, 1), (1, 0)]), off)]
  transfers between devices with their start and end apart: 7 -> 5, of which waited for: 4 -> 3; matrix products, arithmetic and copies ran while one was open for 1% -> 0% of each run, Pallas kernels for 0% -> 0%
where the time goes in v2:
time: 122 us
  blocking collectives  67.2 us (55%)
  starting transfers between devices  33.9 us (28%)
  Pallas kernels  11.8 us (10%)
  waiting for transfers between devices  5.4 us (4%)
  local copies, waits for them, and re-layouts  1.67 us (1%)
  other arithmetic  1.22 us (1%)
    all_to_all x1, blocking collectives, per_device(): got = lax.all_to_all(send, 'y', 0, 0, tiled=True)  28 us
    all_to_all x1, blocking collectives, per_device(): mine = lax.all_to_all(flat, first, 0, 0, tiled=True).sum(0)  22.9 us
    ppermute x2, starting transfers between devices, both_sides(): return (lax.ppermute(slab, 'core', [(0, 1), (1, 0)]), off)  21.3 us
    all_to_all x1, blocking collectives, per_device(): back = lax.all_to_all(spread, GRID, 0, 0, tiled=True)  16.3 us
    pallas_call x4, Pallas kernels, call(): pl.pallas_call(body, out_shape=[jax.ShapeDtypeStruct(s, jnp.float32) for...  11.8 us
    ppermute x2, starting transfers between devices, both_sides(): off = lax.ppermute(slab, GRID, outer)  7.31 us
    ppermute x1, starting transfers between devices, per_device(): unext = lax.ppermute(edge, GRID, down)  5.33 us
    ppermute x2, waiting for transfers between devices, both_sides(): return (lax.ppermute(slab, 'core', [(0, 1), (1, 0)]), off)  3.06 us
  transfers between devices with their start and end apart: 5, of which 3 were waited for; matrix products, arithmetic and copies ran while one was open for 0% of the time, Pallas kernels for 0%

profile of v2, /device:TPU:1, one launch (start us, length us, event | category | flops | bytes accessed | tf_op | source)
XLA Modules:
  0.0 122.0 jit_solution(2548337645129133263)
XLA Ops:
  0.6 1.1 pad_maximum_fusion.own.fown
  1.7 5.4 %collective-permute-start.1 = (f32[17,4,16,128]{3,2,1,0:T(8,128)S(1)}, f32[17,4,16,128]{3,2,1,0:T(8,128)S(1)}, u32[]{:S(2)}, u32[]{:S(2)}) collective-permute-start(f32[17,4,16,128]{3,2,1,0:T(8,128)S(1)} %pad_maximum_fusion.own.fown), channel_id=1, source_target_pairs={{0,504},{8,16},{16,8},{24,32},{32,24},{40,48},{48,40},{56,64},{64,... | collective-permute-start | bytes 1671176 | tf_op jit(solution)/shard_map/ppermute | solution.py:132
  7.1 10.6 %collective-permute-start = (f32[17,4,16,128]{3,2,1,0:T(8,128)S(1)}, f32[17,4,16,128]{3,2,1,0:T(8,128)S(1)}, u32[]{:S(2)}, u32[]{:S(2)}) collective-permute-start(f32[17,4,16,128]{3,2,1,0:T(8,128)S(1)} %pad_maximum_fusion.own.fown), channel_id=1, source_target_pairs={{0,8},{8,0},{1,9},{9,1},{2,10},{10,2},{3,11},{11,3},{4,12},{12,4},... | collective-permute-start | bytes 1671176 | tf_op jit(solution)/shard_map/ppermute | solution.py:133
  17.8 0.0 collective-permute-done.1.off
  17.8 1.6 %collective-permute-done.on = f32[17,4,16,128]{3,2,1,0:T(8,128)S(1)} collective-permute-done((f32[17,4,16,128]{3,2,1,0:T(8,128)S(1)}, f32[17,4,16,128]{3,2,1,0:T(8,128)S(1)}, u32[]{:S(2)}, u32[]{:S(2)}) %collective-permute-start) | collective-permute-done | bytes 557088 | tf_op jit(solution)/shard_map/ppermute | solution.py:133
  19.3 3.5 %shard_map.49 = (f32[16,4,16,128]{3,2,1,0:T(8,128)S(1)}, f32[8,16,128]{2,1,0:T(8,128)S(1)}) custom-call(f32[17,4,16,128]{3,2,1,0:T(8,128)S(1)} %pad_maximum_fusion.own.fown, f32[17,4,16,128]{3,2,1,0:T(8,128)S(1)} %collective-permute-done.on, f32[17,4,16,128]{3,2,1,0:T(8,128)S(1)} %collective-permute-done.1.off), custom_call_target="tpu_custom_call" | custom-call | tf_op jit(solution)/shard_map/pallas_call | solution.py:114
  22.8 1.9 %collective-permute-start.3 = (f32[16,4,16,128]{3,2,1,0:T(8,128)S(1)}, f32[16,4,16,128]{3,2,1,0:T(8,128)S(1)}, u32[]{:S(2)}, u32[]{:S(2)}) collective-permute-start(f32[16,4,16,128]{3,2,1,0:T(8,128)S(1)} %get-tuple-element.7.gown), channel_id=1, source_target_pairs={{0,504},{8,16},{16,8},{24,32},{32,24},{40,48},{48,40},{56,64},{64,... | collective-permute-start | bytes 1572872 | tf_op jit(solution)/shard_map/ppermute | solution.py:132
  24.7 10.7 %collective-permute-start.2 = (f32[16,4,16,128]{3,2,1,0:T(8,128)S(1)}, f32[16,4,16,128]{3,2,1,0:T(8,128)S(1)}, u32[]{:S(2)}, u32[]{:S(2)}) collective-permute-start(f32[16,4,16,128]{3,2,1,0:T(8,128)S(1)} %get-tuple-element.7.gown), channel_id=1, source_target_pairs={{0,8},{8,0},{1,9},{9,1},{2,10},{10,2},{3,11},{11,3},{4,12},{12,4},... | collective-permute-start | bytes 1572872 | tf_op jit(solution)/shard_map/ppermute | solution.py:133
  35.4 0.0 collective-permute-done.3.off
  35.4 1.5 %collective-permute-done.2.on = f32[16,4,16,128]{3,2,1,0:T(8,128)S(1)} collective-permute-done((f32[16,4,16,128]{3,2,1,0:T(8,128)S(1)}, f32[16,4,16,128]{3,2,1,0:T(8,128)S(1)}, u32[]{:S(2)}, u32[]{:S(2)}) %collective-permute-start.2) | collective-permute-done | bytes 524320 | tf_op jit(solution)/shard_map/ppermute | solution.py:133
  36.9 4.3 %shard_map.50 = (f32[16,4,16,128]{3,2,1,0:T(8,128)}, f32[16,2,16,128]{3,2,1,0:T(8,128)S(1)}) custom-call(f32[16,4,16,128]{3,2,1,0:T(8,128)S(1)} %get-tuple-element.7.gown, f32[16,4,16,128]{3,2,1,0:T(8,128)S(1)} %collective-permute-done.2.on, f32[16,4,16,128]{3,2,1,0:T(8,128)S(1)} %collective-permute-done.3.off, ...), custom_call_target="tpu_custom_call" | custom-call | tf_op jit(solution)/shard_map/pallas_call | solution.py:114
  41.2 5.3 %collective-permute-start.4 = (f32[16,2,16,128]{3,2,1,0:T(8,128)S(1)}, f32[16,2,16,128]{3,2,1,0:T(8,128)S(1)}, u32[]{:S(2)}, u32[]{:S(2)}) collective-permute-start(f32[16,2,16,128]{3,2,1,0:T(8,128)S(1)} %get-tuple-element.10), channel_id=1, source_target_pairs={{0,504},{8,0},{16,8},{24,16},{32,24},{40,32},{48,40},{56,48},{64,5... | collective-permute-start | bytes 786440 | tf_op jit(solution)/shard_map/ppermute | solution.py:141
  46.5 2.3 %collective-permute-done.4.unext = f32[16,2,16,128]{3,2,1,0:T(8,128)S(1)} collective-permute-done((f32[16,2,16,128]{3,2,1,0:T(8,128)S(1)}, f32[16,2,16,128]{3,2,1,0:T(8,128)S(1)}, u32[]{:S(2)}, u32[]{:S(2)}) %collective-permute-start.4) | collective-permute-done | bytes 262176 | tf_op jit(solution)/shard_map/ppermute | solution.py:141
  48.9 0.0 copy-start
  48.9 1.0 copy-done
  49.9 1.7 %shard_map.51 = f32[8,2,8,16,128]{4,3,2,1,0:T(8,128)S(1)} custom-call(f32[16,4,16,128]{3,2,1,0:T(8,128)S(1)} %copy-done, f32[16,2,16,128]{3,2,1,0:T(8,128)S(1)} %collective-permute-done.4.unext, f32[8,16,128]{2,1,0:T(8,128)S(1)} %get-tuple-element.8.diag), custom_call_target="tpu_custom_call" | custom-call | tf_op jit(solution)/shard_map/pallas_call | solution.py:114
  51.7 28.0 %all_to_all.15.blocks = f32[8,2,8,16,128]{4,3,2,1,0:T(8,128)S(1)} all-to-all(f32[8,2,8,16,128]{4,3,2,1,0:T(8,128)S(1)} %shard_map.51), channel_id=1, replica_groups=mesh['x'=4,'z'=8,'core'=2,'y'=8] {'y'}, dimensions={0} | all-to-all | bytes 2097152 | tf_op jit(solution)/shard_map/all_to_all | solution.py:143
  79.7 2.3 %shard_map.52 = f32[8,2,16,128]{3,2,1,0:T(8,128)S(1)} custom-call(f32[8,2,8,16,128]{4,3,2,1,0:T(8,128)S(1)} %all_to_all.15.blocks), custom_call_target="tpu_custom_call" | custom-call | tf_op jit(solution)/shard_map/pallas_call | solution.py:114
  82.0 22.9 %all_to_all.16 = f32[64,4,128]{2,1,0:T(4,128)S(1)} all-to-all(f32[64,4,128]{2,1,0:T(4,128)S(1)} %bitcast.5), channel_id=1, replica_groups=mesh['x'=4,'z'=8,'core'=2,'y'=8] {'y','x','core'}, dimensions={0} | all-to-all | bytes 262144 | tf_op jit(solution)/shard_map/all_to_all | solution.py:149
  104.9 0.1 reduce_sum.18
  105.0 16.3 %all_to_all.17 = f32[64,4,128]{2,1,0:T(4,128)S(1)} all-to-all(f32[64,4,128]{2,1,0:T(4,128)S(1)} %broadcast_in_dim.10), channel_id=1, replica_groups=mesh['x'=4,'z'=8,'core'=2,'y'=8] {'x','z','core'}, dimensions={0} | all-to-all | bytes 262144 | tf_op jit(solution)/shard_map/all_to_all | solution.py:151
  121.4 0.6 fusion
  (3 shorter events, 0.1 us)
Async XLA Ops:
  1.7 16.0 %collective-permute-start.1 = (f32[17,4,16,128]{3,2,1,0:T(8,128)S(1)}, f32[17,4,16,128]{3,2,1,0:T(8,128)S(1)}, u32[]{:S(2)}, u32[]{:S(2)}) collective-permute-start(f32[17,4,16,128]{3,2,1,0:T(8,128)S(1)} %pad_maximum_fusion.own.fown), channel_id=1, source_target_pairs={{0,504},{8,16},{16,8},{24,32},{32,24},{40,48},{48,40},{56,64},{64,... | collective-permute-start | bytes 1671176 | tf_op jit(solution)/shard_map/ppermute | solution.py:132
  7.1 12.2 %collective-permute-start = (f32[17,4,16,128]{3,2,1,0:T(8,128)S(1)}, f32[17,4,16,128]{3,2,1,0:T(8,128)S(1)}, u32[]{:S(2)}, u32[]{:S(2)}) collective-permute-start(f32[17,4,16,128]{3,2,1,0:T(8,128)S(1)} %pad_maximum_fusion.own.fown), channel_id=1, source_target_pairs={{0,8},{8,0},{1,9},{9,1},{2,10},{10,2},{3,11},{11,3},{4,12},{12,4},... | collective-permute-start | bytes 1671176 | tf_op jit(solution)/shard_map/ppermute | solution.py:133
  22.8 12.6 %collective-permute-start.3 = (f32[16,4,16,128]{3,2,1,0:T(8,128)S(1)}, f32[16,4,16,128]{3,2,1,0:T(8,128)S(1)}, u32[]{:S(2)}, u32[]{:S(2)}) collective-permute-start(f32[16,4,16,128]{3,2,1,0:T(8,128)S(1)} %get-tuple-element.7.gown), channel_id=1, source_target_pairs={{0,504},{8,16},{16,8},{24,32},{32,24},{40,48},{48,40},{56,64},{64,... | collective-permute-start | bytes 1572872 | tf_op jit(solution)/shard_map/ppermute | solution.py:132
  24.7 12.2 %collective-permute-start.2 = (f32[16,4,16,128]{3,2,1,0:T(8,128)S(1)}, f32[16,4,16,128]{3,2,1,0:T(8,128)S(1)}, u32[]{:S(2)}, u32[]{:S(2)}) collective-permute-start(f32[16,4,16,128]{3,2,1,0:T(8,128)S(1)} %get-tuple-element.7.gown), channel_id=1, source_target_pairs={{0,8},{8,0},{1,9},{9,1},{2,10},{10,2},{3,11},{11,3},{4,12},{12,4},... | collective-permute-start | bytes 1572872 | tf_op jit(solution)/shard_map/ppermute | solution.py:133
  41.2 7.7 %collective-permute-start.4 = (f32[16,2,16,128]{3,2,1,0:T(8,128)S(1)}, f32[16,2,16,128]{3,2,1,0:T(8,128)S(1)}, u32[]{:S(2)}, u32[]{:S(2)}) collective-permute-start(f32[16,2,16,128]{3,2,1,0:T(8,128)S(1)} %get-tuple-element.10), channel_id=1, source_target_pairs={{0,504},{8,0},{16,8},{24,16},{32,24},{40,32},{48,40},{56,48},{64,5... | collective-permute-start | bytes 786440 | tf_op jit(solution)/shard_map/ppermute | solution.py:141
  48.9 1.0 copy-start

commit v3 on v2

--- a/solution.py
+++ b/solution.py
@@ -55,68 +55,114 @@
     by_core(run, on, off)
 
 
-def stage_two(gown, on, off, fown, diag, out, edge):
+def stage_two(gown, on, off, fown, diag, out, send, half_diag):
+    orbs, planes, rows, lanes = gown.shape
+    peers, depth, octet, _ = send.shape
+    chunk = lanes // peers
+    half = 0.5 * (HALF_WIDTH * diag[2:-2] + SHIFT_MID)
+    half_diag[...] = jnp.concatenate([half.reshape(planes * rows, lanes)] * 2, axis=0).T
+
     def run(lo, hi):
-        def step(o, carry):
-            g = jnp.concatenate([lo[o], gown[o], hi[o]], axis=0)
-            first = scaled_op(g, diag[...])
-            u = 4.0 * scaled_op(first, diag[2:-2]) - 2.0 * gown[o] - fown[o]
-            out[o] = u
-            edge[o] = u[:2]
+        def step(p, carry):
+            pair = []
+            for o in (p, p + octet):
+                g = jnp.concatenate([lo[o], gown[o], hi[o]], axis=0)
+                first = scaled_op(g, diag[...])
+                u = 4.0 * scaled_op(first, diag[2:-2]) - 2.0 * gown[o] - fown[o]
+                out[o] = u
+                pair.append(u.reshape(planes * rows, lanes))
+            lines = jnp.concatenate(pair, axis=0).T
+            for k in range(peers):
+                at = (k + 1) % peers * chunk
+                send[k, :chunk, pl.ds(p, 1), :] = lines[k * chunk : (k + 1) * chunk][:, None, :]
+                send[k, chunk:, pl.ds(p, 1), :] = lines[at : at + depth - chunk][:, None, :]
             return carry
 
-        lax.fori_loop(0, gown.shape[0], step, 0)
+        lax.fori_loop(0, octet, step, 0)
 
     by_core(run, on, off)
 
 
-def stage_half(uown, unext, diag, out):
-    orbs, planes, rows, lanes = uown.shape
-    half_diag = 0.5 * (HALF_WIDTH * diag[2:-2] + SHIFT_MID)
-
-    def step(o, carry):
-        u = uown[o]
-        up = jnp.concatenate([u, unext[o]], axis=0)
-        near = up[1:-1] + pltpu.roll(u, rows - 1, 1) + pltpu.roll(u, lanes - 1, 2)
-        far = up[2:] + pltpu.roll(u, rows - 2, 1) + pltpu.roll(u, lanes - 2, 2)
-        w = half_diag * u + NEAR * near + FAR * far
-        for plane in range(planes):
-            for part in range(rows // 8):
-                peer = plane * (rows // 8) + part
-                out[peer, 0, :, pl.ds(o, 1), :] = u[plane, part * 8 : part * 8 + 8][:, None, :]
-                out[peer, 1, :, pl.ds(o, 1), :] = w[plane, part * 8 : part * 8 + 8][:, None, :]
-        return carry
-
-    lax.fori_loop(0, orbs, step, 0)
-
-
-def gram(blocks, out):
-    bands, _, rows, orbs, lanes = blocks.shape
-    total = bands * orbs
+def lane_ids(like):
+    return lax.broadcasted_iota(jnp.int32, like.shape, 2)
+
+
+def pack_edge(got, out):
+    for j in range(out.shape[0]):
+        a, b = got[:, 2 * j], got[:, 2 * j + 1]
+        out[j] = jnp.where(lane_ids(a) % 64 < 32, a, pltpu.roll(b, 32, 2))
+
+
+def split(x):
+    high = x.astype(jnp.bfloat16)
+    return high, (x - high.astype(jnp.float32)).astype(jnp.bfloat16)
+
+
+def dot3(a, b):
     dims = (((1,), (1,)), ((), ()))
-
-    def dot(a, b):
-        return lax.dot_general(a, b, dims, precision=lax.Precision.HIGHEST, preferred_element_type=jnp.float32)
-
-    over = jnp.zeros((total, total), jnp.float32)
-    half = jnp.zeros((total, total), jnp.float32)
-    for row in range(rows):
-        f = blocks[:, 0, row].reshape(total, lanes)
-        w = blocks[:, 1, row].reshape(total, lanes)
-        over = over + dot(f, f)
-        half = half + dot(f, w)
-    ham = half + half.T
-    out[:, 0] = over.reshape(bands, orbs, total)
-    out[:, 1] = ham.reshape(bands, orbs, total)
-
-
-def call(body, out_shapes, *args):
+    (ah, al), (bh, bl) = a, b
+    parts = [
+        lax.dot_general(x, y, dims, preferred_element_type=jnp.float32) for x, y in ((ah, bh), (ah, bl), (al, bh))
+    ]
+    return parts[0] + (parts[1] + parts[2])
+
+
+def orbital_rows(a, b):
+    low = lane_ids(a) < 64
+    top = jnp.where(low, a, pltpu.roll(b, 64, 2))
+    end = jnp.where(low, pltpu.roll(a, 64, 2), b)
+    return jnp.stack([top, end], axis=1).reshape(-1, a.shape[-1])
+
+
+def gram_own(got, half_diag, over, half):
+    bands, depth, octet, _ = got.shape
+    start = pl.multiple_of(lax.axis_index("y") * (depth - 2), 16)
+    x = lane_ids(got[:, 0]) % 16
+    z = lane_ids(got[:, 0]) % 64 // 16
+
+    def one_sided(y):
+        u = got[:, y]
+        near = got[:, y + 1] + jnp.where(x < 15, pltpu.roll(u, 127, 2), pltpu.roll(u, 15, 2))
+        far = got[:, y + 2] + jnp.where(x < 14, pltpu.roll(u, 126, 2), pltpu.roll(u, 14, 2))
+        near = near + jnp.where(z < 3, pltpu.roll(u, 112, 2), 0.0)
+        far = far + jnp.where(z < 2, pltpu.roll(u, 96, 2), 0.0)
+        return half_diag[pl.ds(start + y, 1), :][None] * u + NEAR * near + FAR * far
+
+    total_over, total_half = 0.0, 0.0
+    for y in range(0, depth - 2, 2):
+        u = split(orbital_rows(got[:, y], got[:, y + 1]))
+        w = split(orbital_rows(one_sided(y), one_sided(y + 1)))
+        total_over = total_over + dot3(u, u)
+        total_half = total_half + dot3(u, w)
+    over[...] = total_over
+    half[...] = total_half
+
+
+def gram_edge(got, edge, over, half, out):
+    bands, depth, octet, _ = got.shape
+    z = lane_ids(edge[0]) % 64 // 16
+    total = half[...]
+    for j in range(edge.shape[0]):
+        e = edge[j]
+        by_y = []
+        for near, far in ((48, 32), (16, 0)):
+            one = jnp.where(z == 3, pltpu.roll(e, near, 2), 0.0)
+            two = jnp.where(z >= 2, pltpu.roll(e, far, 2) if far else e, 0.0)
+            by_y.append(NEAR * one + FAR * two)
+        u = split(orbital_rows(got[:, 2 * j], got[:, 2 * j + 1]))
+        total = total + dot3(u, split(orbital_rows(*by_y)))
+    out[:, 0] = over[...].reshape(bands, -1, total.shape[-1])
+    out[:, 1] = (total + total.T).reshape(bands, -1, total.shape[-1])
+
+
+def call(body, out_shapes, *args, flops=0):
     return pl.pallas_call(
         body,
         out_shape=[jax.ShapeDtypeStruct(s, jnp.float32) for s in out_shapes],
         in_specs=[VMEM] * len(args),
         out_specs=[VMEM] * len(out_shapes),
         compiler_params=LIMIT,
+        cost_estimate=pl.CostEstimate(flops=flops, bytes_accessed=1 << 20, transcendentals=0),
     )(*args)
 
 
@@ -134,14 +180,20 @@
 
     slab = jnp.concatenate([orbitals, potential[None]], axis=0)
     g, diag = call(stage_one, [orbitals.shape, (planes + 4, rows, lanes)], slab, *both_sides(slab))
-    u, edge = call(
-        stage_two, [orbitals.shape, (orbs, 2, rows, lanes)], g, *both_sides(g), slab, diag
+    total = bands * orbs
+    u, send, half_diag = call(
+        stage_two,
+        [orbitals.shape, (bands, lanes // bands + 2, orbs // 2, 2 * planes * rows), (lanes, 2 * planes * rows)],
+        g,
+        *both_sides(g),
+        slab,
+        diag,
     )
-
-    unext = lax.ppermute(edge, GRID, down)
-    (send,) = call(stage_half, [(bands, 2, planes * rows // bands, orbs, lanes)], u, unext, diag)
     got = lax.all_to_all(send, "y", 0, 0, tiled=True)
-    (part,) = call(gram, [(bands, 2, orbs, bands * orbs)], got)
+    (edge,) = call(pack_edge, [(lanes // bands // 2, bands, orbs // 2, 2 * planes * rows)], got)
+    edge = lax.ppermute(edge, GRID, down)
+    over, half = call(gram_own, [(total, total)] * 2, got, half_diag, flops=1 << 30)
+    (part,) = call(gram_edge, [(bands, 2, orbs, total)], got, edge, over, half)
 
     first = ("y", "x", "core")
     pieces = lax.axis_size(first)

time: 122 us -> 110 us (0.902)
  blocking collectives: 67.2 us -> 57.3 us
  waiting for transfers between devices: 5.4 us -> 3.06 us
  starting transfers between devices: 33.9 us -> 36.1 us
    all_to_all x1, blocking collectives: 28 us -> 20.9 us  [per_device(): got = lax.all_to_all(send, 'y', 0, 0, tiled=True)]
    all_to_all x1, blocking collectives: 22.9 us -> 19.2 us  [per_device(): mine = lax.all_to_all(flat, first, 0, 0, tiled=True).sum(0)]
    ppermute x1, waiting for transfers between devices: 2.34 us -> 0.01 us  [per_device(): edge = lax.ppermute(edge, GRID, down)]
    ppermute x1, starting transfers between devices: 5.33 us -> 7.47 us  [per_device(): edge = lax.ppermute(edge, GRID, down)]
    pallas_call x4 -> x5, Pallas kernels: 11.8 us -> 10.8 us  [call(): pl.pallas_call(body, out_shape=[jax.ShapeDtypeStruct(s, jnp.float32) for...]
  transfers between devices with their start and end apart: 5 -> 5, of which waited for: 3 -> 2; matrix products, arithmetic and copies ran while one was open for 0% -> 0% of each run, Pallas kernels for 0% -> 2%
where the time goes in v3:
time: 110 us
  blocking collectives  57.3 us (52%)
  starting transfers between devices  36.1 us (33%)
  Pallas kernels  10.8 us (10%)
  waiting for transfers between devices  3.06 us (3%)
  other arithmetic  1.22 us (1%)
    ppermute x2, starting transfers between devices, both_sides(): return (lax.ppermute(slab, 'core', [(0, 1), (1, 0)]), off)  21.3 us
    all_to_all x1, blocking collectives, per_device(): got = lax.all_to_all(send, 'y', 0, 0, tiled=True)  20.9 us
    all_to_all x1, blocking collectives, per_device(): mine = lax.all_to_all(flat, first, 0, 0, tiled=True).sum(0)  19.2 us
    all_to_all x1, blocking collectives, per_device(): back = lax.all_to_all(spread, GRID, 0, 0, tiled=True)  17.3 us
    pallas_call x5, Pallas kernels, call(): pl.pallas_call(body, out_shape=[jax.ShapeDtypeStruct(s, jnp.float32) for...  10.8 us
    ppermute x1, starting transfers between devices, per_device(): edge = lax.ppermute(edge, GRID, down)  7.47 us
    ppermute x2, starting transfers between devices, both_sides(): off = lax.ppermute(slab, GRID, outer)  7.31 us
    ppermute x2, waiting for transfers between devices, both_sides(): return (lax.ppermute(slab, 'core', [(0, 1), (1, 0)]), off)  3.06 us
  transfers between devices with their start and end apart: 5, of which 2 were waited for; matrix products, arithmetic and copies ran while one was open for 0% of the time, Pallas kernels for 2%

profile of v3, /device:TPU:1, one launch (start us, length us, event | category | flops | bytes accessed | tf_op | source)
XLA Modules:
  0.0 109.8 jit_solution(11898261027325179037)
XLA Ops:
  0.6 1.1 %pad_maximum_fusion.own.fown = f32[17,4,16,128]{3,2,1,0:T(8,128)S(1)} fusion(f32[1,4,16,128]{3,2,1,0:T(8,128)} %bitcast.7, f32[16,4,16,128]{3,2,1,0:T(8,128)} %param.2), kind=kLoop, calls=%fused_computation | loop fusion | flops 139264 | bytes 1114112 | tf_op jit(solution)/shard_map/concatenate | solution.py:181
  1.7 5.4 %collective-permute-start.1 = (f32[17,4,16,128]{3,2,1,0:T(8,128)S(1)}, f32[17,4,16,128]{3,2,1,0:T(8,128)S(1)}, u32[]{:S(2)}, u32[]{:S(2)}) collective-permute-start(f32[17,4,16,128]{3,2,1,0:T(8,128)S(1)} %pad_maximum_fusion.own.fown), channel_id=1, source_target_pairs={{0,504},{8,16},{16,8},{24,32},{32,24},{40,48},{48,40},{56,64},{64,... | collective-permute-start | bytes 1671176 | tf_op jit(solution)/shard_map/ppermute | solution.py:178
  7.1 10.6 %collective-permute-start = (f32[17,4,16,128]{3,2,1,0:T(8,128)S(1)}, f32[17,4,16,128]{3,2,1,0:T(8,128)S(1)}, u32[]{:S(2)}, u32[]{:S(2)}) collective-permute-start(f32[17,4,16,128]{3,2,1,0:T(8,128)S(1)} %pad_maximum_fusion.own.fown), channel_id=1, source_target_pairs={{0,8},{8,0},{1,9},{9,1},{2,10},{10,2},{3,11},{11,3},{4,12},{12,4},... | collective-permute-start | bytes 1671176 | tf_op jit(solution)/shard_map/ppermute | solution.py:179
  17.8 0.0 collective-permute-done.1.off
  17.8 1.6 %collective-permute-done.on = f32[17,4,16,128]{3,2,1,0:T(8,128)S(1)} collective-permute-done((f32[17,4,16,128]{3,2,1,0:T(8,128)S(1)}, f32[17,4,16,128]{3,2,1,0:T(8,128)S(1)}, u32[]{:S(2)}, u32[]{:S(2)}) %collective-permute-start) | collective-permute-done | bytes 557088 | tf_op jit(solution)/shard_map/ppermute | solution.py:179
  19.3 3.5 %shard_map.49 = (f32[16,4,16,128]{3,2,1,0:T(8,128)S(1)}, f32[8,16,128]{2,1,0:T(8,128)S(1)}) custom-call(f32[17,4,16,128]{3,2,1,0:T(8,128)S(1)} %pad_maximum_fusion.own.fown, f32[17,4,16,128]{3,2,1,0:T(8,128)S(1)} %collective-permute-done.on, f32[17,4,16,128]{3,2,1,0:T(8,128)S(1)} %collective-permute-done.1.off), custom_call_target="tpu_custom_call" | custom-call | bytes 1048576 | tf_op jit(solution)/shard_map/pallas_call | solution.py:159
  22.8 1.9 %collective-permute-start.3 = (f32[16,4,16,128]{3,2,1,0:T(8,128)S(1)}, f32[16,4,16,128]{3,2,1,0:T(8,128)S(1)}, u32[]{:S(2)}, u32[]{:S(2)}) collective-permute-start(f32[16,4,16,128]{3,2,1,0:T(8,128)S(1)} %get-tuple-element.10.gown), channel_id=1, source_target_pairs={{0,504},{8,16},{16,8},{24,32},{32,24},{40,48},{48,40},{56,64},{64,... | collective-permute-start | bytes 1572872 | tf_op jit(solution)/shard_map/ppermute | solution.py:178
  24.7 10.7 %collective-permute-start.2 = (f32[16,4,16,128]{3,2,1,0:T(8,128)S(1)}, f32[16,4,16,128]{3,2,1,0:T(8,128)S(1)}, u32[]{:S(2)}, u32[]{:S(2)}) collective-permute-start(f32[16,4,16,128]{3,2,1,0:T(8,128)S(1)} %get-tuple-element.10.gown), channel_id=1, source_target_pairs={{0,8},{8,0},{1,9},{9,1},{2,10},{10,2},{3,11},{11,3},{4,12},{12,4},... | collective-permute-start | bytes 1572872 | tf_op jit(solution)/shard_map/ppermute | solution.py:179
  35.4 0.0 collective-permute-done.3.off
  35.4 1.5 %collective-permute-done.2.on = f32[16,4,16,128]{3,2,1,0:T(8,128)S(1)} collective-permute-done((f32[16,4,16,128]{3,2,1,0:T(8,128)S(1)}, f32[16,4,16,128]{3,2,1,0:T(8,128)S(1)}, u32[]{:S(2)}, u32[]{:S(2)}) %collective-permute-start.2) | collective-permute-done | bytes 524320 | tf_op jit(solution)/shard_map/ppermute | solution.py:179
  36.9 4.3 %shard_map.50 = (f32[16,4,16,128]{3,2,1,0:T(8,128)}, f32[8,18,8,128]{3,2,1,0:T(8,128)S(1)}, f32[128,128]{1,0:T(8,128)S(1)}) custom-call(f32[16,4,16,128]{3,2,1,0:T(8,128)S(1)} %get-tuple-element.10.gown, f32[16,4,16,128]{3,2,1,0:T(8,128)S(1)} %collective-permute-done.2.on, f32[16,4,16,128]{3,2,1,0:T(8,128)S(1)} %collective-permute-done.3.off, ...), custom_call_target="tpu_custom_call" | custom-call | bytes 1048576 | tf_op jit(solution)/shard_map/pallas_call | solution.py:159
  41.3 20.9 %all_to_all.15.got = f32[8,18,8,128]{3,2,1,0:T(8,128)S(1)} all-to-all(f32[8,18,8,128]{3,2,1,0:T(8,128)S(1)} %get-tuple-element.13), channel_id=1, replica_groups=mesh['x'=4,'z'=8,'core'=2,'y'=8] {'y'}, dimensions={0} | all-to-all | bytes 1179648 | tf_op jit(solution)/shard_map/all_to_all | solution.py:192
  62.2 0.1 shard_map.51
  62.3 7.5 %collective-permute-start.4 = (f32[8,8,8,128]{3,2,1,0:T(8,128)S(1)}, f32[8,8,8,128]{3,2,1,0:T(8,128)S(1)}, u32[]{:S(2)}, u32[]{:S(2)}) collective-permute-start(f32[8,8,8,128]{3,2,1,0:T(8,128)S(1)} %shard_map.51), channel_id=1, source_target_pairs={{0,504},{8,0},{16,8},{24,16},{32,24},{40,32},{48,40},{56,48},{64,5... | collective-permute-start | bytes 786440 | tf_op jit(solution)/shard_map/ppermute | solution.py:194
  69.8 1.8 %shard_map.52 = (f32[128,128]{1,0:T(8,128)S(1)}, f32[128,128]{1,0:T(8,128)S(1)}) custom-call(f32[8,18,8,128]{3,2,1,0:T(8,128)S(1)} %all_to_all.15.got, f32[128,128]{1,0:T(8,128)S(1)} %get-tuple-element.14.half_diag), custom_call_target="tpu_custom_call" | custom-call | flops 1073741824 | bytes 1048576 | tf_op jit(solution)/shard_map/pallas_call | solution.py:159
  71.6 0.0 collective-permute-done.4.edge
  71.6 1.0 shard_map.53
  72.6 19.2 %all_to_all.16 = f32[64,4,128]{2,1,0:T(4,128)S(1)} all-to-all(f32[64,4,128]{2,1,0:T(4,128)S(1)} %bitcast.5), channel_id=1, replica_groups=mesh['x'=4,'z'=8,'core'=2,'y'=8] {'y','x','core'}, dimensions={0} | all-to-all | bytes 262144 | tf_op jit(solution)/shard_map/all_to_all | solution.py:201
  91.8 0.1 reduce_sum.18
  91.9 17.3 %all_to_all.17 = f32[64,4,128]{2,1,0:T(4,128)S(1)} all-to-all(f32[64,4,128]{2,1,0:T(4,128)S(1)} %broadcast_in_dim.10), channel_id=1, replica_groups=mesh['x'=4,'z'=8,'core'=2,'y'=8] {'x','z','core'}, dimensions={0} | all-to-all | bytes 262144 | tf_op jit(solution)/shard_map/all_to_all | solution.py:203
  109.2 0.6 fusion
  (3 shorter events, 0.1 us)
Async XLA Ops:
  1.7 16.0 %collective-permute-start.1 = (f32[17,4,16,128]{3,2,1,0:T(8,128)S(1)}, f32[17,4,16,128]{3,2,1,0:T(8,128)S(1)}, u32[]{:S(2)}, u32[]{:S(2)}) collective-permute-start(f32[17,4,16,128]{3,2,1,0:T(8,128)S(1)} %pad_maximum_fusion.own.fown), channel_id=1, source_target_pairs={{0,504},{8,16},{16,8},{24,32},{32,24},{40,48},{48,40},{56,64},{64,... | collective-permute-start | bytes 1671176 | tf_op jit(solution)/shard_map/ppermute | solution.py:178
  7.1 12.2 %collective-permute-start = (f32[17,4,16,128]{3,2,1,0:T(8,128)S(1)}, f32[17,4,16,128]{3,2,1,0:T(8,128)S(1)}, u32[]{:S(2)}, u32[]{:S(2)}) collective-permute-start(f32[17,4,16,128]{3,2,1,0:T(8,128)S(1)} %pad_maximum_fusion.own.fown), channel_id=1, source_target_pairs={{0,8},{8,0},{1,9},{9,1},{2,10},{10,2},{3,11},{11,3},{4,12},{12,4},... | collective-permute-start | bytes 1671176 | tf_op jit(solution)/shard_map/ppermute | solution.py:179
  22.8 12.6 %collective-permute-start.3 = (f32[16,4,16,128]{3,2,1,0:T(8,128)S(1)}, f32[16,4,16,128]{3,2,1,0:T(8,128)S(1)}, u32[]{:S(2)}, u32[]{:S(2)}) collective-permute-start(f32[16,4,16,128]{3,2,1,0:T(8,128)S(1)} %get-tuple-element.10.gown), channel_id=1, source_target_pairs={{0,504},{8,16},{16,8},{24,32},{32,24},{40,48},{48,40},{56,64},{64,... | collective-permute-start | bytes 1572872 | tf_op jit(solution)/shard_map/ppermute | solution.py:178
  24.7 12.2 %collective-permute-start.2 = (f32[16,4,16,128]{3,2,1,0:T(8,128)S(1)}, f32[16,4,16,128]{3,2,1,0:T(8,128)S(1)}, u32[]{:S(2)}, u32[]{:S(2)}) collective-permute-start(f32[16,4,16,128]{3,2,1,0:T(8,128)S(1)} %get-tuple-element.10.gown), channel_id=1, source_target_pairs={{0,8},{8,0},{1,9},{9,1},{2,10},{10,2},{3,11},{11,3},{4,12},{12,4},... | collective-permute-start | bytes 1572872 | tf_op jit(solution)/shard_map/ppermute | solution.py:179
  62.3 9.3 %collective-permute-start.4 = (f32[8,8,8,128]{3,2,1,0:T(8,128)S(1)}, f32[8,8,8,128]{3,2,1,0:T(8,128)S(1)}, u32[]{:S(2)}, u32[]{:S(2)}) collective-permute-start(f32[8,8,8,128]{3,2,1,0:T(8,128)S(1)} %shard_map.51), channel_id=1, source_target_pairs={{0,504},{8,0},{16,8},{24,16},{32,24},{40,32},{48,40},{56,48},{64,5... | collective-permute-start | bytes 786440 | tf_op jit(solution)/shard_map/ppermute | solution.py:194

commit v4 on v3

--- a/solution.py
+++ b/solution.py
@@ -11,6 +11,7 @@
 NEAR = -16.0 / 24.0
 FAR = 1.0 / 24.0
 GRID = ("x", "z", "core")
+SIDE = 4
 VMEM = pl.BlockSpec(memory_space=pltpu.VMEM)
 LIMIT = pltpu.CompilerParams(vmem_limit_bytes=24 * 1024 * 1024)
 
@@ -44,13 +45,14 @@
         v = jnp.concatenate([lo[orbs, 2:], own[orbs], hi[orbs, :2]], axis=0)
         diag[...] = (v + (DIAG - SHIFT_MID)) / HALF_WIDTH
 
-        def step(o, carry):
-            f = jnp.concatenate([lo[o], own[o], hi[o]], axis=0)
-            first = scaled_op(f, diag[...])
-            out[o] = 2.0 * scaled_op(first, diag[2:-2]) - own[o]
+        def step(group, carry):
+            members = [group * SIDE + i for i in range(SIDE)]
+            firsts = [scaled_op(jnp.concatenate([lo[o], own[o], hi[o]], axis=0), diag[...]) for o in members]
+            for o, first in zip(members, firsts):
+                out[o] = 2.0 * scaled_op(first, diag[2:-2]) - own[o]
             return carry
 
-        lax.fori_loop(0, orbs, step, 0)
+        lax.fori_loop(0, orbs // SIDE, step, 0)
 
     by_core(run, on, off)
 
@@ -63,22 +65,24 @@
     half_diag[...] = jnp.concatenate([half.reshape(planes * rows, lanes)] * 2, axis=0).T
 
     def run(lo, hi):
-        def step(p, carry):
-            pair = []
-            for o in (p, p + octet):
-                g = jnp.concatenate([lo[o], gown[o], hi[o]], axis=0)
-                first = scaled_op(g, diag[...])
+        def step(group, carry):
+            octets = [group * (SIDE // 2) + i for i in range(SIDE // 2)]
+            members = [o for p in octets for o in (p, p + octet)]
+            firsts = [scaled_op(jnp.concatenate([lo[o], gown[o], hi[o]], axis=0), diag[...]) for o in members]
+            us = []
+            for o, first in zip(members, firsts):
                 u = 4.0 * scaled_op(first, diag[2:-2]) - 2.0 * gown[o] - fown[o]
                 out[o] = u
-                pair.append(u.reshape(planes * rows, lanes))
-            lines = jnp.concatenate(pair, axis=0).T
-            for k in range(peers):
-                at = (k + 1) % peers * chunk
-                send[k, :chunk, pl.ds(p, 1), :] = lines[k * chunk : (k + 1) * chunk][:, None, :]
-                send[k, chunk:, pl.ds(p, 1), :] = lines[at : at + depth - chunk][:, None, :]
+                us.append(u.reshape(planes * rows, lanes))
+            for i, p in enumerate(octets):
+                lines = jnp.concatenate(us[2 * i : 2 * i + 2], axis=0).T
+                for k in range(peers):
+                    at = (k + 1) % peers * chunk
+                    send[k, :chunk, pl.ds(p, 1), :] = lines[k * chunk : (k + 1) * chunk][:, None, :]
+                    send[k, chunk:, pl.ds(p, 1), :] = lines[at : at + depth - chunk][:, None, :]
             return carry
 
-        lax.fori_loop(0, octet, step, 0)
+        lax.fori_loop(0, 2 * octet // SIDE, step, 0)
 
     by_core(run, on, off)
 
@@ -90,7 +94,7 @@
 def pack_edge(got, out):
     for j in range(out.shape[0]):
         a, b = got[:, 2 * j], got[:, 2 * j + 1]
-        out[j] = jnp.where(lane_ids(a) % 64 < 32, a, pltpu.roll(b, 32, 2))
+        out[j] = jnp.where(lane_ids(a) % 64 < 32, pltpu.roll(a, 96, 2), b)
 
 
 def split(x):
@@ -114,18 +118,19 @@
     return jnp.stack([top, end], axis=1).reshape(-1, a.shape[-1])
 
 
-def gram_own(got, half_diag, over, half):
+def gram_own(got, half_diag, over, half, first):
     bands, depth, octet, _ = got.shape
     start = pl.multiple_of(lax.axis_index("y") * (depth - 2), 16)
-    x = lane_ids(got[:, 0]) % 16
-    z = lane_ids(got[:, 0]) % 64 // 16
+    lane = lane_ids(got[:, 0])
+    x = lane % 16
+    z = lane % 64 // 16
 
     def one_sided(y):
         u = got[:, y]
         near = got[:, y + 1] + jnp.where(x < 15, pltpu.roll(u, 127, 2), pltpu.roll(u, 15, 2))
         far = got[:, y + 2] + jnp.where(x < 14, pltpu.roll(u, 126, 2), pltpu.roll(u, 14, 2))
-        near = near + jnp.where(z < 3, pltpu.roll(u, 112, 2), 0.0)
-        far = far + jnp.where(z < 2, pltpu.roll(u, 96, 2), 0.0)
+        near = near + jnp.where(z >= 1, pltpu.roll(u, 16, 2), 0.0)
+        far = far + jnp.where(z >= 2, pltpu.roll(u, 32, 2), 0.0)
         return half_diag[pl.ds(start + y, 1), :][None] * u + NEAR * near + FAR * far
 
     total_over, total_half = 0.0, 0.0
@@ -136,21 +141,22 @@
         total_half = total_half + dot3(u, w)
     over[...] = total_over
     half[...] = total_half
-
-
-def gram_edge(got, edge, over, half, out):
-    bands, depth, octet, _ = got.shape
-    z = lane_ids(edge[0]) % 64 // 16
+    for j in range(first.shape[0]):
+        two = []
+        for y in (4 * j, 4 * j + 2):
+            two.append(jnp.where(lane % 64 < 32, got[:, y], pltpu.roll(got[:, y + 1], 32, 2)))
+        first[j] = orbital_rows(*two)
+
+
+def gram_edge(edge, first, over, half, out):
+    bands = edge.shape[1]
+    third = lane_ids(edge[0]) % 32 < 16
     total = half[...]
-    for j in range(edge.shape[0]):
-        e = edge[j]
-        by_y = []
-        for near, far in ((48, 32), (16, 0)):
-            one = jnp.where(z == 3, pltpu.roll(e, near, 2), 0.0)
-            two = jnp.where(z >= 2, pltpu.roll(e, far, 2) if far else e, 0.0)
-            by_y.append(NEAR * one + FAR * two)
-        u = split(orbital_rows(got[:, 2 * j], got[:, 2 * j + 1]))
-        total = total + dot3(u, split(orbital_rows(*by_y)))
+    for j in range(first.shape[0]):
+        two = []
+        for e in (edge[2 * j], edge[2 * j + 1]):
+            two.append(FAR * e + jnp.where(third, NEAR * pltpu.roll(e, 112, 2), 0.0))
+        total = total + dot3(split(first[j]), split(orbital_rows(*two)))
     out[:, 0] = over[...].reshape(bands, -1, total.shape[-1])
     out[:, 1] = (total + total.T).reshape(bands, -1, total.shape[-1])
 
@@ -171,7 +177,7 @@
     slabs = lax.axis_size(GRID)
     bands = lax.axis_size("y")
     cells_all = slabs * planes * rows * lanes
-    down = ring_shift(slabs, -1)
+    following = ring_shift(slabs, 1)
     outer = [(i, (i + (1 if i % 2 else -1)) % slabs) for i in range(slabs)]
 
     def both_sides(slab):
@@ -191,14 +197,15 @@
     )
     got = lax.all_to_all(send, "y", 0, 0, tiled=True)
     (edge,) = call(pack_edge, [(lanes // bands // 2, bands, orbs // 2, 2 * planes * rows)], got)
-    edge = lax.ppermute(edge, GRID, down)
-    over, half = call(gram_own, [(total, total)] * 2, got, half_diag, flops=1 << 30)
-    (part,) = call(gram_edge, [(bands, 2, orbs, total)], got, edge, over, half)
-
-    first = ("y", "x", "core")
-    pieces = lax.axis_size(first)
+    edge = lax.ppermute(edge, GRID, following)
+    firsts = (lanes // bands // 4, total, 2 * planes * rows)
+    over, half, first = call(gram_own, [(total, total), (total, total), firsts], got, half_diag, flops=1 << 30)
+    (part,) = call(gram_edge, [(bands, 2, orbs, total)], edge, first, over, half)
+
+    reducers = ("y", "x", "core")
+    pieces = lax.axis_size(reducers)
     flat = part.reshape(pieces, -1, bands * orbs)
-    mine = lax.all_to_all(flat, first, 0, 0, tiled=True).sum(0)
+    mine = lax.all_to_all(flat, reducers, 0, 0, tiled=True).sum(0)
     spread = jnp.broadcast_to(mine[None], (slabs, *mine.shape))
     back = lax.all_to_all(spread, GRID, 0, 0, tiled=True)
     nx, nz, nc = (lax.axis_size(a) for a in GRID)

time: 110 us -> 107 us (0.973)
  starting transfers between devices: 36.1 us -> 30.5 us
  waiting for transfers between devices: 3.06 us -> 7.63 us
  Pallas kernels: 10.8 us -> 7.89 us
    ppermute x1, starting transfers between devices: 7.47 us -> 1.92 us  [per_device(): edge = lax.ppermute(edge, GRID, following)]
    ppermute x1, waiting for transfers between devices: 0.01 us -> 4.57 us  [per_device(): edge = lax.ppermute(edge, GRID, following)]
    all_to_all x1, blocking collectives: 19.2 us -> 22.7 us  [per_device(): mine = lax.all_to_all(flat, reducers, 0, 0, tiled=True).sum(0)]
    all_to_all x1, blocking collectives: 17.3 us -> 14.1 us  [per_device(): back = lax.all_to_all(spread, GRID, 0, 0, tiled=True)]
    pallas_call x5, Pallas kernels: 10.8 us -> 7.89 us  [call(): pl.pallas_call(body, out_shape=[jax.ShapeDtypeStruct(s, jnp.float32) for...]
  transfers between devices with their start and end apart: 5 -> 5, of which waited for: 2 -> 3; matrix products, arithmetic and copies ran while one was open for 0% -> 0% of each run, Pallas kernels for 2% -> 2%
where the time goes in v4:
time: 107 us; the launch traced here: 106 us
  blocking collectives  57.7 us (54%)
  starting transfers between devices  30.5 us (29%)
  Pallas kernels  7.89 us (7%)
  waiting for transfers between devices  7.63 us (7%)
  other arithmetic  1.22 us (1%)
    all_to_all x1, blocking collectives, per_device(): mine = lax.all_to_all(flat, reducers, 0, 0, tiled=True).sum(0)  22.7 us
    ppermute x2, starting transfers between devices, both_sides(): return (lax.ppermute(slab, 'core', [(0, 1), (1, 0)]), off)  21.3 us
    all_to_all x1, blocking collectives, per_device(): got = lax.all_to_all(send, 'y', 0, 0, tiled=True)  20.9 us
    all_to_all x1, blocking collectives, per_device(): back = lax.all_to_all(spread, GRID, 0, 0, tiled=True)  14.1 us
    pallas_call x5, Pallas kernels, call(): pl.pallas_call(body, out_shape=[jax.ShapeDtypeStruct(s, jnp.float32) for...  7.89 us
    ppermute x2, starting transfers between devices, both_sides(): off = lax.ppermute(slab, GRID, outer)  7.31 us
    ppermute x1, waiting for transfers between devices, per_device(): edge = lax.ppermute(edge, GRID, following)  4.57 us
    ppermute x2, waiting for transfers between devices, both_sides(): return (lax.ppermute(slab, 'core', [(0, 1), (1, 0)]), off)  3.06 us
  transfers between devices with their start and end apart: 5, of which 3 were waited for; matrix products, arithmetic and copies ran while one was open for 0% of the time, Pallas kernels for 2%

profile of v4, /device:TPU:1, one launch (start us, length us, event | category | flops | bytes accessed | tf_op | source)
XLA Modules:
  0.0 106.3 jit_solution(5577920447842132825)
XLA Ops:
  0.6 1.1 %pad_maximum_fusion.own.fown = f32[17,4,16,128]{3,2,1,0:T(8,128)S(1)} fusion(f32[1,4,16,128]{3,2,1,0:T(8,128)} %bitcast.7, f32[16,4,16,128]{3,2,1,0:T(8,128)} %param.2), kind=kLoop, calls=%fused_computation | loop fusion | flops 139264 | bytes 1114112 | tf_op jit(solution)/shard_map/concatenate | solution.py:187
  1.7 5.4 %collective-permute-start.1 = (f32[17,4,16,128]{3,2,1,0:T(8,128)S(1)}, f32[17,4,16,128]{3,2,1,0:T(8,128)S(1)}, u32[]{:S(2)}, u32[]{:S(2)}) collective-permute-start(f32[17,4,16,128]{3,2,1,0:T(8,128)S(1)} %pad_maximum_fusion.own.fown), channel_id=1, source_target_pairs={{0,504},{8,16},{16,8},{24,32},{32,24},{40,48},{48,40},{56,64},{64,... | collective-permute-start | bytes 1671176 | tf_op jit(solution)/shard_map/ppermute | solution.py:184
  7.1 10.6 %collective-permute-start = (f32[17,4,16,128]{3,2,1,0:T(8,128)S(1)}, f32[17,4,16,128]{3,2,1,0:T(8,128)S(1)}, u32[]{:S(2)}, u32[]{:S(2)}) collective-permute-start(f32[17,4,16,128]{3,2,1,0:T(8,128)S(1)} %pad_maximum_fusion.own.fown), channel_id=1, source_target_pairs={{0,8},{8,0},{1,9},{9,1},{2,10},{10,2},{3,11},{11,3},{4,12},{12,4},... | collective-permute-start | bytes 1671176 | tf_op jit(solution)/shard_map/ppermute | solution.py:185
  17.8 0.0 collective-permute-done.1.off
  17.8 1.6 %collective-permute-done.on = f32[17,4,16,128]{3,2,1,0:T(8,128)S(1)} collective-permute-done((f32[17,4,16,128]{3,2,1,0:T(8,128)S(1)}, f32[17,4,16,128]{3,2,1,0:T(8,128)S(1)}, u32[]{:S(2)}, u32[]{:S(2)}) %collective-permute-start) | collective-permute-done | bytes 557088 | tf_op jit(solution)/shard_map/ppermute | solution.py:185
  19.3 1.9 %shard_map.49 = (f32[16,4,16,128]{3,2,1,0:T(8,128)S(1)}, f32[8,16,128]{2,1,0:T(8,128)S(1)}) custom-call(f32[17,4,16,128]{3,2,1,0:T(8,128)S(1)} %pad_maximum_fusion.own.fown, f32[17,4,16,128]{3,2,1,0:T(8,128)S(1)} %collective-permute-done.on, f32[17,4,16,128]{3,2,1,0:T(8,128)S(1)} %collective-permute-done.1.off), custom_call_target="tpu_custom_call" | custom-call | bytes 1048576 | tf_op jit(solution)/shard_map/pallas_call | solution.py:165
  21.3 1.9 %collective-permute-start.3 = (f32[16,4,16,128]{3,2,1,0:T(8,128)S(1)}, f32[16,4,16,128]{3,2,1,0:T(8,128)S(1)}, u32[]{:S(2)}, u32[]{:S(2)}) collective-permute-start(f32[16,4,16,128]{3,2,1,0:T(8,128)S(1)} %get-tuple-element.11.gown), channel_id=1, source_target_pairs={{0,504},{8,16},{16,8},{24,32},{32,24},{40,48},{48,40},{56,64},{64,... | collective-permute-start | bytes 1572872 | tf_op jit(solution)/shard_map/ppermute | solution.py:184
  23.2 10.7 %collective-permute-start.2 = (f32[16,4,16,128]{3,2,1,0:T(8,128)S(1)}, f32[16,4,16,128]{3,2,1,0:T(8,128)S(1)}, u32[]{:S(2)}, u32[]{:S(2)}) collective-permute-start(f32[16,4,16,128]{3,2,1,0:T(8,128)S(1)} %get-tuple-element.11.gown), channel_id=1, source_target_pairs={{0,8},{8,0},{1,9},{9,1},{2,10},{10,2},{3,11},{11,3},{4,12},{12,4},... | collective-permute-start | bytes 1572872 | tf_op jit(solution)/shard_map/ppermute | solution.py:185
  33.9 0.0 collective-permute-done.3.off
  33.9 1.5 %collective-permute-done.2.on = f32[16,4,16,128]{3,2,1,0:T(8,128)S(1)} collective-permute-done((f32[16,4,16,128]{3,2,1,0:T(8,128)S(1)}, f32[16,4,16,128]{3,2,1,0:T(8,128)S(1)}, u32[]{:S(2)}, u32[]{:S(2)}) %collective-permute-start.2) | collective-permute-done | bytes 524320 | tf_op jit(solution)/shard_map/ppermute | solution.py:185
  35.4 3.2 %shard_map.50 = (f32[16,4,16,128]{3,2,1,0:T(8,128)}, f32[8,18,8,128]{3,2,1,0:T(8,128)S(1)}, f32[128,128]{1,0:T(8,128)S(1)}) custom-call(f32[16,4,16,128]{3,2,1,0:T(8,128)S(1)} %get-tuple-element.11.gown, f32[16,4,16,128]{3,2,1,0:T(8,128)S(1)} %collective-permute-done.2.on, f32[16,4,16,128]{3,2,1,0:T(8,128)S(1)} %collective-permute-done.3.off, ...), custom_call_target="tpu_custom_call" | custom-call | bytes 1048576 | tf_op jit(solution)/shard_map/pallas_call | solution.py:165
  38.6 20.9 %all_to_all.15.got = f32[8,18,8,128]{3,2,1,0:T(8,128)S(1)} all-to-all(f32[8,18,8,128]{3,2,1,0:T(8,128)S(1)} %get-tuple-element.14), channel_id=1, replica_groups=mesh['x'=4,'z'=8,'core'=2,'y'=8] {'y'}, dimensions={0} | all-to-all | bytes 1179648 | tf_op jit(solution)/shard_map/all_to_all | solution.py:198
  59.5 0.1 shard_map.51
  59.6 1.9 %collective-permute-start.4 = (f32[8,8,8,128]{3,2,1,0:T(8,128)S(1)}, f32[8,8,8,128]{3,2,1,0:T(8,128)S(1)}, u32[]{:S(2)}, u32[]{:S(2)}) collective-permute-start(f32[8,8,8,128]{3,2,1,0:T(8,128)S(1)} %shard_map.51), channel_id=1, source_target_pairs={{0,8},{8,16},{16,24},{24,32},{32,40},{40,48},{48,56},{56,64},{64,7... | collective-permute-start | bytes 786440 | tf_op jit(solution)/shard_map/ppermute | solution.py:200
  61.6 2.0 %shard_map.52 = (f32[128,128]{1,0:T(8,128)S(1)}, f32[128,128]{1,0:T(8,128)S(1)}, f32[4,128,128]{2,1,0:T(8,128)S(1)}) custom-call(f32[8,18,8,128]{3,2,1,0:T(8,128)S(1)} %all_to_all.15.got, f32[128,128]{1,0:T(8,128)S(1)} %get-tuple-element.15.half_diag), custom_call_target="tpu_custom_call" | custom-call | flops 1073741824 | bytes 1048576 | tf_op jit(solution)/shard_map/pallas_call | solution.py:165
  63.6 4.6 %collective-permute-done.4.edge = f32[8,8,8,128]{3,2,1,0:T(8,128)S(1)} collective-permute-done((f32[8,8,8,128]{3,2,1,0:T(8,128)S(1)}, f32[8,8,8,128]{3,2,1,0:T(8,128)S(1)}, u32[]{:S(2)}, u32[]{:S(2)}) %collective-permute-start.4) | collective-permute-done | bytes 262176 | tf_op jit(solution)/shard_map/ppermute | solution.py:200
  68.1 0.6 shard_map.53
  68.8 22.7 %all_to_all.16 = f32[64,4,128]{2,1,0:T(4,128)S(1)} all-to-all(f32[64,4,128]{2,1,0:T(4,128)S(1)} %bitcast.5), channel_id=1, replica_groups=mesh['x'=4,'z'=8,'core'=2,'y'=8] {'y','x','core'}, dimensions={0} | all-to-all | bytes 262144 | tf_op jit(solution)/shard_map/all_to_all | solution.py:208
  91.4 0.1 reduce_sum.18
  91.5 14.1 %all_to_all.17 = f32[64,4,128]{2,1,0:T(4,128)S(1)} all-to-all(f32[64,4,128]{2,1,0:T(4,128)S(1)} %broadcast_in_dim.10), channel_id=1, replica_groups=mesh['x'=4,'z'=8,'core'=2,'y'=8] {'x','z','core'}, dimensions={0} | all-to-all | bytes 262144 | tf_op jit(solution)/shard_map/all_to_all | solution.py:210
  105.7 0.6 fusion
  (3 shorter events, 0.1 us)
Async XLA Ops:
  1.7 16.0 %collective-permute-start.1 = (f32[17,4,16,128]{3,2,1,0:T(8,128)S(1)}, f32[17,4,16,128]{3,2,1,0:T(8,128)S(1)}, u32[]{:S(2)}, u32[]{:S(2)}) collective-permute-start(f32[17,4,16,128]{3,2,1,0:T(8,128)S(1)} %pad_maximum_fusion.own.fown), channel_id=1, source_target_pairs={{0,504},{8,16},{16,8},{24,32},{32,24},{40,48},{48,40},{56,64},{64,... | collective-permute-start | bytes 1671176 | tf_op jit(solution)/shard_map/ppermute | solution.py:184
  7.1 12.2 %collective-permute-start = (f32[17,4,16,128]{3,2,1,0:T(8,128)S(1)}, f32[17,4,16,128]{3,2,1,0:T(8,128)S(1)}, u32[]{:S(2)}, u32[]{:S(2)}) collective-permute-start(f32[17,4,16,128]{3,2,1,0:T(8,128)S(1)} %pad_maximum_fusion.own.fown), channel_id=1, source_target_pairs={{0,8},{8,0},{1,9},{9,1},{2,10},{10,2},{3,11},{11,3},{4,12},{12,4},... | collective-permute-start | bytes 1671176 | tf_op jit(solution)/shard_map/ppermute | solution.py:185
  21.3 12.6 %collective-permute-start.3 = (f32[16,4,16,128]{3,2,1,0:T(8,128)S(1)}, f32[16,4,16,128]{3,2,1,0:T(8,128)S(1)}, u32[]{:S(2)}, u32[]{:S(2)}) collective-permute-start(f32[16,4,16,128]{3,2,1,0:T(8,128)S(1)} %get-tuple-element.11.gown), channel_id=1, source_target_pairs={{0,504},{8,16},{16,8},{24,32},{32,24},{40,48},{48,40},{56,64},{64,... | collective-permute-start | bytes 1572872 | tf_op jit(solution)/shard_map/ppermute | solution.py:184
  23.2 12.2 %collective-permute-start.2 = (f32[16,4,16,128]{3,2,1,0:T(8,128)S(1)}, f32[16,4,16,128]{3,2,1,0:T(8,128)S(1)}, u32[]{:S(2)}, u32[]{:S(2)}) collective-permute-start(f32[16,4,16,128]{3,2,1,0:T(8,128)S(1)} %get-tuple-element.11.gown), channel_id=1, source_target_pairs={{0,8},{8,0},{1,9},{9,1},{2,10},{10,2},{3,11},{11,3},{4,12},{12,4},... | collective-permute-start | bytes 1572872 | tf_op jit(solution)/shard_map/ppermute | solution.py:185
  59.6 8.5 %collective-permute-start.4 = (f32[8,8,8,128]{3,2,1,0:T(8,128)S(1)}, f32[8,8,8,128]{3,2,1,0:T(8,128)S(1)}, u32[]{:S(2)}, u32[]{:S(2)}) collective-permute-start(f32[8,8,8,128]{3,2,1,0:T(8,128)S(1)} %shard_map.51), channel_id=1, source_target_pairs={{0,8},{8,16},{16,24},{24,32},{32,40},{40,48},{48,56},{56,64},{64,7... | collective-permute-start | bytes 786440 | tf_op jit(solution)/shard_map/ppermute | solution.py:200

commit v5 on v4

--- a/solution.py
+++ b/solution.py
@@ -11,7 +11,8 @@
 NEAR = -16.0 / 24.0
 FAR = 1.0 / 24.0
 GRID = ("x", "z", "core")
-SIDE = 4
+REDUCERS = ("y", "x")
+SIDE = 8
 VMEM = pl.BlockSpec(memory_space=pltpu.VMEM)
 LIMIT = pltpu.CompilerParams(vmem_limit_bytes=24 * 1024 * 1024)
 
@@ -118,7 +119,9 @@
     return jnp.stack([top, end], axis=1).reshape(-1, a.shape[-1])
 
 
-def gram_own(got, half_diag, over, half, first):
+def gram_own(got, half_diag, u, over, half, first, kept, done):
+    keep = pltpu.make_async_copy(u, kept, done)
+    keep.start()
     bands, depth, octet, _ = got.shape
     start = pl.multiple_of(lax.axis_index("y") * (depth - 2), 16)
     lane = lane_ids(got[:, 0])
@@ -146,6 +149,7 @@
         for y in (4 * j, 4 * j + 2):
             two.append(jnp.where(lane % 64 < 32, got[:, y], pltpu.roll(got[:, y + 1], 32, 2)))
         first[j] = orbital_rows(*two)
+    keep.wait()
 
 
 def gram_edge(edge, first, over, half, out):
@@ -161,12 +165,14 @@
     out[:, 1] = (total + total.T).reshape(bands, -1, total.shape[-1])
 
 
-def call(body, out_shapes, *args, flops=0):
+def call(body, out_shapes, *args, kept=0, scratch=(), flops=0):
+    places = [VMEM] * (len(out_shapes) - kept) + [pl.BlockSpec(memory_space=pl.ANY)] * kept
     return pl.pallas_call(
         body,
         out_shape=[jax.ShapeDtypeStruct(s, jnp.float32) for s in out_shapes],
         in_specs=[VMEM] * len(args),
-        out_specs=[VMEM] * len(out_shapes),
+        out_specs=places,
+        scratch_shapes=scratch,
         compiler_params=LIMIT,
         cost_estimate=pl.CostEstimate(flops=flops, bytes_accessed=1 << 20, transcendentals=0),
     )(*args)
@@ -199,17 +205,25 @@
     (edge,) = call(pack_edge, [(lanes // bands // 2, bands, orbs // 2, 2 * planes * rows)], got)
     edge = lax.ppermute(edge, GRID, following)
     firsts = (lanes // bands // 4, total, 2 * planes * rows)
-    over, half, first = call(gram_own, [(total, total), (total, total), firsts], got, half_diag, flops=1 << 30)
+    over, half, first, u = call(
+        gram_own,
+        [(total, total), (total, total), firsts, u.shape],
+        got,
+        half_diag,
+        u,
+        kept=1,
+        scratch=[pltpu.SemaphoreType.DMA],
+        flops=1 << 30,
+    )
     (part,) = call(gram_edge, [(bands, 2, orbs, total)], edge, first, over, half)
 
-    reducers = ("y", "x", "core")
-    pieces = lax.axis_size(reducers)
+    pieces = lax.axis_size(REDUCERS)
     flat = part.reshape(pieces, -1, bands * orbs)
-    mine = lax.all_to_all(flat, reducers, 0, 0, tiled=True).sum(0)
-    spread = jnp.broadcast_to(mine[None], (slabs, *mine.shape))
-    back = lax.all_to_all(spread, GRID, 0, 0, tiled=True)
-    nx, nz, nc = (lax.axis_size(a) for a in GRID)
-    both = back.reshape(nx, nz, nc, *mine.shape).sum(1) / cells_all
+    mine = lax.all_to_all(flat, REDUCERS, 0, 0, tiled=True).sum(0)
+    mine = lax.psum(mine, "core")
+    spread = jnp.broadcast_to(mine[None], (slabs // 2, *mine.shape))
+    back = lax.all_to_all(spread, ("x", "z"), 0, 0, tiled=True)
+    both = back.reshape(lax.axis_size("x"), lax.axis_size("z"), *mine.shape).sum(1) / cells_all
     both = both.reshape(2, orbs, bands * orbs)
     return u, both[0], both[1]
 

time: 107 us -> 105 us (0.981)
    all_to_all x2, blocking collectives: 36.8 us -> 24.5 us  [the longest x1 12.4 us: per_device(): mine = lax.all_to_all(flat, REDUCERS, 0, 0, tiled=True).sum(0)]
    psum x0 -> x1, blocking collectives: none -> 11.4 us  [per_device(): mine = lax.psum(mine, 'core')]
where the time goes in v5:
time: 105 us; the launch traced here: 104 us
  blocking collectives  56.8 us (54%)
  starting transfers between devices  30.5 us (29%)
  waiting for transfers between devices  7.61 us (7%)
  Pallas kernels  6.84 us (7%)
  other arithmetic  1.16 us (1%)
    ppermute x2, starting transfers between devices, both_sides(): return (lax.ppermute(slab, 'core', [(0, 1), (1, 0)]), off)  21.3 us
    all_to_all x1, blocking collectives, per_device(): got = lax.all_to_all(send, 'y', 0, 0, tiled=True)  20.9 us
    all_to_all x1, blocking collectives, per_device(): mine = lax.all_to_all(flat, REDUCERS, 0, 0, tiled=True).sum(0)  12.4 us
    all_to_all x1, blocking collectives, per_device(): back = lax.all_to_all(spread, ('x', 'z'), 0, 0, tiled=True)  12.1 us
    psum x1, blocking collectives, per_device(): mine = lax.psum(mine, 'core')  11.4 us
    ppermute x2, starting transfers between devices, both_sides(): off = lax.ppermute(slab, GRID, outer)  7.31 us
    pallas_call x5, Pallas kernels, call(): pl.pallas_call(body, out_shape=[jax.ShapeDtypeStruct(s, jnp.float32) for...  6.84 us
    ppermute x1, waiting for transfers between devices, per_device(): edge = lax.ppermute(edge, GRID, following)  4.55 us
  transfers between devices with their start and end apart: 5, of which 3 were waited for; matrix products, arithmetic and copies ran while one was open for 0% of the time, Pallas kernels for 2%

profile of v5, /device:TPU:1, one launch (start us, length us, event | category | flops | bytes accessed | tf_op | source)
XLA Modules:
  0.0 104.3 jit_solution(6011026541461771956)
XLA Ops:
  0.6 1.1 %pad_maximum_fusion.own.fown = f32[17,4,16,128]{3,2,1,0:T(8,128)S(1)} fusion(f32[1,4,16,128]{3,2,1,0:T(8,128)} %bitcast.9, f32[16,4,16,128]{3,2,1,0:T(8,128)} %param.2), kind=kLoop, calls=%fused_computation | loop fusion | flops 139264 | bytes 1114112 | tf_op jit(solution)/shard_map/concatenate | solution.py:193
  1.7 5.4 %collective-permute-start.1 = (f32[17,4,16,128]{3,2,1,0:T(8,128)S(1)}, f32[17,4,16,128]{3,2,1,0:T(8,128)S(1)}, u32[]{:S(2)}, u32[]{:S(2)}) collective-permute-start(f32[17,4,16,128]{3,2,1,0:T(8,128)S(1)} %pad_maximum_fusion.own.fown), channel_id=1, source_target_pairs={{0,504},{8,16},{16,8},{24,32},{32,24},{40,48},{48,40},{56,64},{64,... | collective-permute-start | bytes 1671176 | tf_op jit(solution)/shard_map/ppermute | solution.py:190
  7.1 10.6 %collective-permute-start = (f32[17,4,16,128]{3,2,1,0:T(8,128)S(1)}, f32[17,4,16,128]{3,2,1,0:T(8,128)S(1)}, u32[]{:S(2)}, u32[]{:S(2)}) collective-permute-start(f32[17,4,16,128]{3,2,1,0:T(8,128)S(1)} %pad_maximum_fusion.own.fown), channel_id=1, source_target_pairs={{0,8},{8,0},{1,9},{9,1},{2,10},{10,2},{3,11},{11,3},{4,12},{12,4},... | collective-permute-start | bytes 1671176 | tf_op jit(solution)/shard_map/ppermute | solution.py:191
  17.8 0.0 collective-permute-done.1.off
  17.8 1.6 %collective-permute-done.on = f32[17,4,16,128]{3,2,1,0:T(8,128)S(1)} collective-permute-done((f32[17,4,16,128]{3,2,1,0:T(8,128)S(1)}, f32[17,4,16,128]{3,2,1,0:T(8,128)S(1)}, u32[]{:S(2)}, u32[]{:S(2)}) %collective-permute-start) | collective-permute-done | bytes 557088 | tf_op jit(solution)/shard_map/ppermute | solution.py:191
  19.3 1.8 %shard_map.49 = (f32[16,4,16,128]{3,2,1,0:T(8,128)S(1)}, f32[8,16,128]{2,1,0:T(8,128)S(1)}) custom-call(f32[17,4,16,128]{3,2,1,0:T(8,128)S(1)} %pad_maximum_fusion.own.fown, f32[17,4,16,128]{3,2,1,0:T(8,128)S(1)} %collective-permute-done.on, f32[17,4,16,128]{3,2,1,0:T(8,128)S(1)} %collective-permute-done.1.off), custom_call_target="tpu_custom_call" | custom-call | bytes 1048576 | tf_op jit(solution)/shard_map/pallas_call | solution.py:170
  21.1 1.9 %collective-permute-start.3 = (f32[16,4,16,128]{3,2,1,0:T(8,128)S(1)}, f32[16,4,16,128]{3,2,1,0:T(8,128)S(1)}, u32[]{:S(2)}, u32[]{:S(2)}) collective-permute-start(f32[16,4,16,128]{3,2,1,0:T(8,128)S(1)} %get-tuple-element.12.gown), channel_id=1, source_target_pairs={{0,504},{8,16},{16,8},{24,32},{32,24},{40,48},{48,40},{56,64},{64,... | collective-permute-start | bytes 1572872 | tf_op jit(solution)/shard_map/ppermute | solution.py:190
  23.1 10.7 %collective-permute-start.2 = (f32[16,4,16,128]{3,2,1,0:T(8,128)S(1)}, f32[16,4,16,128]{3,2,1,0:T(8,128)S(1)}, u32[]{:S(2)}, u32[]{:S(2)}) collective-permute-start(f32[16,4,16,128]{3,2,1,0:T(8,128)S(1)} %get-tuple-element.12.gown), channel_id=1, source_target_pairs={{0,8},{8,0},{1,9},{9,1},{2,10},{10,2},{3,11},{11,3},{4,12},{12,4},... | collective-permute-start | bytes 1572872 | tf_op jit(solution)/shard_map/ppermute | solution.py:191
  33.7 0.0 collective-permute-done.3.off
  33.8 1.5 %collective-permute-done.2.on = f32[16,4,16,128]{3,2,1,0:T(8,128)S(1)} collective-permute-done((f32[16,4,16,128]{3,2,1,0:T(8,128)S(1)}, f32[16,4,16,128]{3,2,1,0:T(8,128)S(1)}, u32[]{:S(2)}, u32[]{:S(2)}) %collective-permute-start.2) | collective-permute-done | bytes 524320 | tf_op jit(solution)/shard_map/ppermute | solution.py:191
  35.3 2.3 %shard_map.50 = (f32[16,4,16,128]{3,2,1,0:T(8,128)S(1)}, f32[8,18,8,128]{3,2,1,0:T(8,128)S(1)}, f32[128,128]{1,0:T(8,128)S(1)}) custom-call(f32[16,4,16,128]{3,2,1,0:T(8,128)S(1)} %get-tuple-element.12.gown, f32[16,4,16,128]{3,2,1,0:T(8,128)S(1)} %collective-permute-done.2.on, f32[16,4,16,128]{3,2,1,0:T(8,128)S(1)} %collective-permute-done.3.off, ...), custom_call_target="tpu_custom_call" | custom-call | bytes 1048576 | tf_op jit(solution)/shard_map/pallas_call | solution.py:170
  37.5 20.9 %all_to_all.15.got = f32[8,18,8,128]{3,2,1,0:T(8,128)S(1)} all-to-all(f32[8,18,8,128]{3,2,1,0:T(8,128)S(1)} %get-tuple-element.14), channel_id=1, replica_groups=mesh['x'=4,'z'=8,'core'=2,'y'=8] {'y'}, dimensions={0} | all-to-all | bytes 1179648 | tf_op jit(solution)/shard_map/all_to_all | solution.py:204
  58.5 0.1 shard_map.52
  58.6 1.9 %collective-permute-start.4 = (f32[8,8,8,128]{3,2,1,0:T(8,128)S(1)}, f32[8,8,8,128]{3,2,1,0:T(8,128)S(1)}, u32[]{:S(2)}, u32[]{:S(2)}) collective-permute-start(f32[8,8,8,128]{3,2,1,0:T(8,128)S(1)} %shard_map.52), channel_id=1, source_target_pairs={{0,8},{8,16},{16,24},{24,32},{32,40},{40,48},{48,56},{56,64},{64,7... | collective-permute-start | bytes 786440 | tf_op jit(solution)/shard_map/ppermute | solution.py:206
  60.5 2.0 %shard_map.51 = (f32[128,128]{1,0:T(8,128)S(1)}, f32[128,128]{1,0:T(8,128)S(1)}, f32[4,128,128]{2,1,0:T(8,128)S(1)}, f32[16,4,16,128]{3,2,1,0:T(8,128)}) custom-call(f32[8,18,8,128]{3,2,1,0:T(8,128)S(1)} %all_to_all.15.got, f32[128,128]{1,0:T(8,128)S(1)} %get-tuple-element.15.half_diag, f32[16,4,16,128]{3,2,1,0:T(8,128)S(1)} %get-tuple-element.16.u), custom_call_target="tpu_custom_call" | custom-call | flops 1073741824 | bytes 1048576 | tf_op jit(solution)/shard_map/pallas_call | solution.py:170
  62.5 4.6 %collective-permute-done.4.edge = f32[8,8,8,128]{3,2,1,0:T(8,128)S(1)} collective-permute-done((f32[8,8,8,128]{3,2,1,0:T(8,128)S(1)}, f32[8,8,8,128]{3,2,1,0:T(8,128)S(1)}, u32[]{:S(2)}, u32[]{:S(2)}) %collective-permute-start.4) | collective-permute-done | bytes 262176 | tf_op jit(solution)/shard_map/ppermute | solution.py:206
  67.1 0.6 shard_map.53
  67.7 12.4 %all_to_all.16 = f32[32,8,128]{2,1,0:T(8,128)S(1)} all-to-all(f32[32,8,128]{2,1,0:T(8,128)S(1)} %bitcast.8), channel_id=1, replica_groups=mesh['x'=4,'z'=8,'core'=2,'y'=8] {'y','x'}, dimensions={0} | all-to-all | bytes 262144 | tf_op jit(solution)/shard_map/all_to_all | solution.py:222
  80.1 11.4 %psum.7 = f32[8,128]{1,0:T(8,128)S(1)} all-reduce(f32[8,128]{1,0:T(8,128)S(1)} %reduce_sum.18), channel_id=1, replica_groups=mesh['x'=4,'z'=8,'core'=2,'y'=8] {'core'}, use_global_device_ids=true, to_apply=%region_1.0 | all-reduce | flops 1024 | bytes 8192 | tf_op jit(solution)/shard_map/psum | solution.py:223
  91.6 12.1 %all_to_all.17 = f32[32,8,128]{2,1,0:T(8,128)S(1)} all-to-all(f32[32,8,128]{2,1,0:T(8,128)S(1)} %broadcast_in_dim.10), channel_id=1, replica_groups=mesh['x'=4,'z'=8,'core'=2,'y'=8] {'x','z'}, dimensions={0} | all-to-all | bytes 262144 | tf_op jit(solution)/shard_map/all_to_all | solution.py:225
  103.7 0.6 slice_bitcast_fusion
  (4 shorter events, 0.1 us)
Async XLA Ops:
  1.7 16.0 %collective-permute-start.1 = (f32[17,4,16,128]{3,2,1,0:T(8,128)S(1)}, f32[17,4,16,128]{3,2,1,0:T(8,128)S(1)}, u32[]{:S(2)}, u32[]{:S(2)}) collective-permute-start(f32[17,4,16,128]{3,2,1,0:T(8,128)S(1)} %pad_maximum_fusion.own.fown), channel_id=1, source_target_pairs={{0,504},{8,16},{16,8},{24,32},{32,24},{40,48},{48,40},{56,64},{64,... | collective-permute-start | bytes 1671176 | tf_op jit(solution)/shard_map/ppermute | solution.py:190
  7.1 12.2 %collective-permute-start = (f32[17,4,16,128]{3,2,1,0:T(8,128)S(1)}, f32[17,4,16,128]{3,2,1,0:T(8,128)S(1)}, u32[]{:S(2)}, u32[]{:S(2)}) collective-permute-start(f32[17,4,16,128]{3,2,1,0:T(8,128)S(1)} %pad_maximum_fusion.own.fown), channel_id=1, source_target_pairs={{0,8},{8,0},{1,9},{9,1},{2,10},{10,2},{3,11},{11,3},{4,12},{12,4},... | collective-permute-start | bytes 1671176 | tf_op jit(solution)/shard_map/ppermute | solution.py:191
  21.1 12.6 %collective-permute-start.3 = (f32[16,4,16,128]{3,2,1,0:T(8,128)S(1)}, f32[16,4,16,128]{3,2,1,0:T(8,128)S(1)}, u32[]{:S(2)}, u32[]{:S(2)}) collective-permute-start(f32[16,4,16,128]{3,2,1,0:T(8,128)S(1)} %get-tuple-element.12.gown), channel_id=1, source_target_pairs={{0,504},{8,16},{16,8},{24,32},{32,24},{40,48},{48,40},{56,64},{64,... | collective-permute-start | bytes 1572872 | tf_op jit(solution)/shard_map/ppermute | solution.py:190
  23.1 12.2 %collective-permute-start.2 = (f32[16,4,16,128]{3,2,1,0:T(8,128)S(1)}, f32[16,4,16,128]{3,2,1,0:T(8,128)S(1)}, u32[]{:S(2)}, u32[]{:S(2)}) collective-permute-start(f32[16,4,16,128]{3,2,1,0:T(8,128)S(1)} %get-tuple-element.12.gown), channel_id=1, source_target_pairs={{0,8},{8,0},{1,9},{9,1},{2,10},{10,2},{3,11},{11,3},{4,12},{12,4},... | collective-permute-start | bytes 1572872 | tf_op jit(solution)/shard_map/ppermute | solution.py:191
  58.6 8.5 %collective-permute-start.4 = (f32[8,8,8,128]{3,2,1,0:T(8,128)S(1)}, f32[8,8,8,128]{3,2,1,0:T(8,128)S(1)}, u32[]{:S(2)}, u32[]{:S(2)}) collective-permute-start(f32[8,8,8,128]{3,2,1,0:T(8,128)S(1)} %shard_map.52), channel_id=1, source_target_pairs={{0,8},{8,16},{16,24},{24,32},{32,40},{40,48},{48,56},{56,64},{64,7... | collective-permute-start | bytes 786440 | tf_op jit(solution)/shard_map/ppermute | solution.py:206

commit v6 on v5

--- a/solution.py
+++ b/solution.py
@@ -21,16 +21,49 @@
     return [(i, (i + by) % size) for i in range(size)]
 
 
-def scaled_op(padded, diag):
-    mid = padded[2:-2]
+def scaled_xy(mid, diag):
     rows, lanes = mid.shape[1], mid.shape[2]
-    near = padded[1:-3] + padded[3:-1]
-    far = padded[:-4] + padded[4:]
-    near = near + (pltpu.roll(mid, 1, 1) + pltpu.roll(mid, rows - 1, 1))
-    far = far + (pltpu.roll(mid, 2, 1) + pltpu.roll(mid, rows - 2, 1))
+    near = pltpu.roll(mid, 1, 1) + pltpu.roll(mid, rows - 1, 1)
+    far = pltpu.roll(mid, 2, 1) + pltpu.roll(mid, rows - 2, 1)
     near = near + (pltpu.roll(mid, 1, 2) + pltpu.roll(mid, lanes - 1, 2))
     far = far + (pltpu.roll(mid, 2, 2) + pltpu.roll(mid, lanes - 2, 2))
     return diag * mid + (NEAR / HALF_WIDTH) * near + (FAR / HALF_WIDTH) * far
+
+
+def scaled_z(padded):
+    near = padded[1:-3] + padded[3:-1]
+    far = padded[:-4] + padded[4:]
+    return (NEAR / HALF_WIDTH) * near + (FAR / HALF_WIDTH) * far
+
+
+def scaled_op(padded, diag):
+    return scaled_xy(padded[2:-2], diag) + scaled_z(padded)
+
+
+def scaled_pot(v):
+    return (v + (DIAG - SHIFT_MID)) / HALF_WIDTH
+
+
+def ahead(own, diag, own_xy):
+    orbs = own_xy.shape[0]
+
+    def step(group, carry):
+        for o in [group * SIDE + i for i in range(SIDE)]:
+            own_xy[o] = scaled_xy(own[o], diag)
+        return carry
+
+    lax.fori_loop(0, orbs // SIDE, step, 0)
+
+
+def ahead_one(own, own_xy):
+    ahead(own, scaled_pot(own[own_xy.shape[0]]), own_xy)
+
+
+def ahead_two(own, diag, own_xy, half_diag):
+    _, planes, rows, lanes = own.shape
+    half = 0.5 * (HALF_WIDTH * diag[2:-2] + SHIFT_MID)
+    half_diag[...] = jnp.concatenate([half.reshape(planes * rows, lanes)] * 2, axis=0).T
+    ahead(own, diag[2:-2], own_xy)
 
 
 def by_core(run, on, off):
@@ -39,16 +72,22 @@
     pl.when(core == 1)(lambda: run(on, off))
 
 
-def stage_one(own, on, off, out, diag):
+def first_op(lo, own, hi, own_xy, diag, o):
+    before, after = scaled_xy(lo[o, 2:], diag[:2]), scaled_xy(hi[o, :2], diag[-2:])
+    return jnp.concatenate([before, own_xy[o], after], axis=0) + scaled_z(
+        jnp.concatenate([lo[o], own[o], hi[o]], axis=0)
+    )
+
+
+def stage_one(own, on, off, own_xy, out, diag):
     orbs = own.shape[0] - 1
 
     def run(lo, hi):
-        v = jnp.concatenate([lo[orbs, 2:], own[orbs], hi[orbs, :2]], axis=0)
-        diag[...] = (v + (DIAG - SHIFT_MID)) / HALF_WIDTH
+        diag[...] = scaled_pot(jnp.concatenate([lo[orbs, 2:], own[orbs], hi[orbs, :2]], axis=0))
 
         def step(group, carry):
             members = [group * SIDE + i for i in range(SIDE)]
-            firsts = [scaled_op(jnp.concatenate([lo[o], own[o], hi[o]], axis=0), diag[...]) for o in members]
+            firsts = [first_op(lo, own, hi, own_xy, diag[...], o) for o in members]
             for o, first in zip(members, firsts):
                 out[o] = 2.0 * scaled_op(first, diag[2:-2]) - own[o]
             return carry
@@ -58,18 +97,16 @@
     by_core(run, on, off)
 
 
-def stage_two(gown, on, off, fown, diag, out, send, half_diag):
+def stage_two(gown, on, off, own_xy, fown, diag, out, send):
     orbs, planes, rows, lanes = gown.shape
     peers, depth, octet, _ = send.shape
     chunk = lanes // peers
-    half = 0.5 * (HALF_WIDTH * diag[2:-2] + SHIFT_MID)
-    half_diag[...] = jnp.concatenate([half.reshape(planes * rows, lanes)] * 2, axis=0).T
 
     def run(lo, hi):
         def step(group, carry):
             octets = [group * (SIDE // 2) + i for i in range(SIDE // 2)]
             members = [o for p in octets for o in (p, p + octet)]
-            firsts = [scaled_op(jnp.concatenate([lo[o], gown[o], hi[o]], axis=0), diag[...]) for o in members]
+            firsts = [first_op(lo, gown, hi, own_xy, diag[...], o) for o in members]
             us = []
             for o, first in zip(members, firsts):
                 u = 4.0 * scaled_op(first, diag[2:-2]) - 2.0 * gown[o] - fown[o]
@@ -191,13 +228,19 @@
         return lax.ppermute(slab, "core", [(0, 1), (1, 0)]), off
 
     slab = jnp.concatenate([orbitals, potential[None]], axis=0)
-    g, diag = call(stage_one, [orbitals.shape, (planes + 4, rows, lanes)], slab, *both_sides(slab))
+    on, off = both_sides(slab)
+    (own_xy,) = call(ahead_one, [orbitals.shape], slab, flops=1 << 28)
+    g, diag = call(stage_one, [orbitals.shape, (planes + 4, rows, lanes)], slab, on, off, own_xy)
+    on, off = both_sides(g)
+    own_xy, half_diag = call(ahead_two, [orbitals.shape, (lanes, 2 * planes * rows)], g, diag, flops=1 << 28)
     total = bands * orbs
-    u, send, half_diag = call(
+    u, send = call(
         stage_two,
-        [orbitals.shape, (bands, lanes // bands + 2, orbs // 2, 2 * planes * rows), (lanes, 2 * planes * rows)],
+        [orbitals.shape, (bands, lanes // bands + 2, orbs // 2, 2 * planes * rows)],
         g,
-        *both_sides(g),
+        on,
+        off,
+        own_xy,
         slab,
         diag,
     )

time: 105 us -> 104 us (level)
  waiting for transfers between devices: 7.61 us -> 6.13 us
    ppermute x2, waiting for transfers between devices: 3.06 us -> 1.57 us  [both_sides(): return (lax.ppermute(slab, 'core', [(0, 1), (1, 0)]), off)]
    pallas_call x5 -> x7, Pallas kernels: 6.84 us -> 7.1 us  [call(): pl.pallas_call(body, out_shape=[jax.ShapeDtypeStruct(s, jnp.float32) for...]
  transfers between devices with their start and end apart: 5 -> 5, of which waited for: 3 -> 3; matrix products, arithmetic and copies ran while one was open for 0% -> 0% of each run, Pallas kernels for 2% -> 3%
where the time goes in v6:
time: 104 us; the launch traced here: 103 us
  blocking collectives  56.8 us (55%)
  starting transfers between devices  30.5 us (29%)
  Pallas kernels  7.1 us (7%)
  waiting for transfers between devices  6.13 us (6%)
  other arithmetic  1.16 us (1%)
    ppermute x2, starting transfers between devices, both_sides(): return (lax.ppermute(slab, 'core', [(0, 1), (1, 0)]), off)  21.3 us
    all_to_all x1, blocking collectives, per_device(): got = lax.all_to_all(send, 'y', 0, 0, tiled=True)  20.9 us
    all_to_all x1, blocking collectives, per_device(): mine = lax.all_to_all(flat, REDUCERS, 0, 0, tiled=True).sum(0)  12.4 us
    all_to_all x1, blocking collectives, per_device(): back = lax.all_to_all(spread, ('x', 'z'), 0, 0, tiled=True)  12.1 us
    psum x1, blocking collectives, per_device(): mine = lax.psum(mine, 'core')  11.4 us
    ppermute x2, starting transfers between devices, both_sides(): off = lax.ppermute(slab, GRID, outer)  7.31 us
    pallas_call x7, Pallas kernels, call(): pl.pallas_call(body, out_shape=[jax.ShapeDtypeStruct(s, jnp.float32) for...  7.1 us
    ppermute x1, waiting for transfers between devices, per_device(): edge = lax.ppermute(edge, GRID, following)  4.56 us
  transfers between devices with their start and end apart: 5, of which 3 were waited for; matrix products, arithmetic and copies ran while one was open for 0% of the time, Pallas kernels for 3%

profile of v6, /device:TPU:1, one launch (start us, length us, event | category | flops | bytes accessed | tf_op | source)
XLA Modules:
  0.0 103.1 jit_solution(13987345577144178854)
XLA Ops:
  0.6 1.1 %pad_maximum_fusion.own.fown = f32[17,4,16,128]{3,2,1,0:T(8,128)S(1)} fusion(f32[1,4,16,128]{3,2,1,0:T(8,128)} %bitcast.9, f32[16,4,16,128]{3,2,1,0:T(8,128)} %param.2), kind=kLoop, calls=%fused_computation | loop fusion | flops 139264 | bytes 1114112 | tf_op jit(solution)/shard_map/concatenate | solution.py:230
  1.7 5.4 %collective-permute-start.1 = (f32[17,4,16,128]{3,2,1,0:T(8,128)S(1)}, f32[17,4,16,128]{3,2,1,0:T(8,128)S(1)}, u32[]{:S(2)}, u32[]{:S(2)}) collective-permute-start(f32[17,4,16,128]{3,2,1,0:T(8,128)S(1)} %pad_maximum_fusion.own.fown), channel_id=1, source_target_pairs={{0,504},{8,16},{16,8},{24,32},{32,24},{40,48},{48,40},{56,64},{64,... | collective-permute-start | bytes 1671176 | tf_op jit(solution)/shard_map/ppermute | solution.py:227
  7.1 10.6 %collective-permute-start = (f32[17,4,16,128]{3,2,1,0:T(8,128)S(1)}, f32[17,4,16,128]{3,2,1,0:T(8,128)S(1)}, u32[]{:S(2)}, u32[]{:S(2)}) collective-permute-start(f32[17,4,16,128]{3,2,1,0:T(8,128)S(1)} %pad_maximum_fusion.own.fown), channel_id=1, source_target_pairs={{0,8},{8,0},{1,9},{9,1},{2,10},{10,2},{3,11},{11,3},{4,12},{12,4},... | collective-permute-start | bytes 1671176 | tf_op jit(solution)/shard_map/ppermute | solution.py:228
  17.8 0.7 shard_map.49.own_xy
  18.4 0.0 collective-permute-done.1.off
  18.5 0.9 collective-permute-done.on
  19.3 1.3 %shard_map.50 = (f32[16,4,16,128]{3,2,1,0:T(8,128)S(1)}, f32[8,16,128]{2,1,0:T(8,128)S(1)}) custom-call(f32[17,4,16,128]{3,2,1,0:T(8,128)S(1)} %pad_maximum_fusion.own.fown, f32[17,4,16,128]{3,2,1,0:T(8,128)S(1)} %collective-permute-done.on, f32[17,4,16,128]{3,2,1,0:T(8,128)S(1)} %collective-permute-done.1.off, f32[16,4,16,128]{3,2,1,0:T(8,128)S(1)} %shard_map.49.own_xy), custom_call_target="tpu_custom_call" | custom-call | bytes 1048576 | tf_op jit(solution)/shard_map/pallas_call | solution.py:207
  20.6 1.9 %collective-permute-start.3 = (f32[16,4,16,128]{3,2,1,0:T(8,128)S(1)}, f32[16,4,16,128]{3,2,1,0:T(8,128)S(1)}, u32[]{:S(2)}, u32[]{:S(2)}) collective-permute-start(f32[16,4,16,128]{3,2,1,0:T(8,128)S(1)} %get-tuple-element.13.own.gown), channel_id=1, source_target_pairs={{0,504},{8,16},{16,8},{24,32},{32,24},{40,48},{48,40},{56,64},{64,... | collective-permute-start | bytes 1572872 | tf_op jit(solution)/shard_map/ppermute | solution.py:227
  22.5 10.7 %collective-permute-start.2 = (f32[16,4,16,128]{3,2,1,0:T(8,128)S(1)}, f32[16,4,16,128]{3,2,1,0:T(8,128)S(1)}, u32[]{:S(2)}, u32[]{:S(2)}) collective-permute-start(f32[16,4,16,128]{3,2,1,0:T(8,128)S(1)} %get-tuple-element.13.own.gown), channel_id=1, source_target_pairs={{0,8},{8,0},{1,9},{9,1},{2,10},{10,2},{3,11},{11,3},{4,12},{12,4},... | collective-permute-start | bytes 1572872 | tf_op jit(solution)/shard_map/ppermute | solution.py:228
  33.2 0.8 shard_map.51
  34.0 0.0 collective-permute-done.3.off
  34.0 0.7 collective-permute-done.2.on
  34.7 1.6 %shard_map.52 = (f32[16,4,16,128]{3,2,1,0:T(8,128)S(1)}, f32[8,18,8,128]{3,2,1,0:T(8,128)S(1)}) custom-call(f32[16,4,16,128]{3,2,1,0:T(8,128)S(1)} %get-tuple-element.13.own.gown, f32[16,4,16,128]{3,2,1,0:T(8,128)S(1)} %collective-permute-done.2.on, f32[16,4,16,128]{3,2,1,0:T(8,128)S(1)} %collective-permute-done.3.off, ...), custom_call_target="tpu_custom_call" | custom-call | bytes 1048576 | tf_op jit(solution)/shard_map/pallas_call | solution.py:207
  36.3 20.9 %all_to_all.15.got = f32[8,18,8,128]{3,2,1,0:T(8,128)S(1)} all-to-all(f32[8,18,8,128]{3,2,1,0:T(8,128)S(1)} %get-tuple-element.16), channel_id=1, replica_groups=mesh['x'=4,'z'=8,'core'=2,'y'=8] {'y'}, dimensions={0} | all-to-all | bytes 1179648 | tf_op jit(solution)/shard_map/all_to_all | solution.py:247
  57.3 0.1 shard_map.54
  57.4 1.9 %collective-permute-start.4 = (f32[8,8,8,128]{3,2,1,0:T(8,128)S(1)}, f32[8,8,8,128]{3,2,1,0:T(8,128)S(1)}, u32[]{:S(2)}, u32[]{:S(2)}) collective-permute-start(f32[8,8,8,128]{3,2,1,0:T(8,128)S(1)} %shard_map.54), channel_id=1, source_target_pairs={{0,8},{8,16},{16,24},{24,32},{32,40},{40,48},{48,56},{56,64},{64,7... | collective-permute-start | bytes 786440 | tf_op jit(solution)/shard_map/ppermute | solution.py:249
  59.3 2.0 %shard_map.53 = (f32[128,128]{1,0:T(8,128)S(1)}, f32[128,128]{1,0:T(8,128)S(1)}, f32[4,128,128]{2,1,0:T(8,128)S(1)}, f32[16,4,16,128]{3,2,1,0:T(8,128)}) custom-call(f32[8,18,8,128]{3,2,1,0:T(8,128)S(1)} %all_to_all.15.got, f32[128,128]{1,0:T(8,128)S(1)} %get-tuple-element.17.half_diag, f32[16,4,16,128]{3,2,1,0:T(8,128)S(1)} %get-tuple-element.18.u), custom_call_target="tpu_custom_call" | custom-call | flops 1073741824 | bytes 1048576 | tf_op jit(solution)/shard_map/pallas_call | solution.py:207
  61.3 4.6 %collective-permute-done.4.edge = f32[8,8,8,128]{3,2,1,0:T(8,128)S(1)} collective-permute-done((f32[8,8,8,128]{3,2,1,0:T(8,128)S(1)}, f32[8,8,8,128]{3,2,1,0:T(8,128)S(1)}, u32[]{:S(2)}, u32[]{:S(2)}) %collective-permute-start.4) | collective-permute-done | bytes 262176 | tf_op jit(solution)/shard_map/ppermute | solution.py:249
  65.9 0.6 shard_map.55
  66.5 12.4 %all_to_all.16 = f32[32,8,128]{2,1,0:T(8,128)S(1)} all-to-all(f32[32,8,128]{2,1,0:T(8,128)S(1)} %bitcast.8), channel_id=1, replica_groups=mesh['x'=4,'z'=8,'core'=2,'y'=8] {'y','x'}, dimensions={0} | all-to-all | bytes 262144 | tf_op jit(solution)/shard_map/all_to_all | solution.py:265
  78.9 11.4 %psum.7 = f32[8,128]{1,0:T(8,128)S(1)} all-reduce(f32[8,128]{1,0:T(8,128)S(1)} %reduce_sum.18), channel_id=1, replica_groups=mesh['x'=4,'z'=8,'core'=2,'y'=8] {'core'}, use_global_device_ids=true, to_apply=%region_1.0 | all-reduce | flops 1024 | bytes 8192 | tf_op jit(solution)/shard_map/psum | solution.py:266
  90.4 12.1 %all_to_all.17 = f32[32,8,128]{2,1,0:T(8,128)S(1)} all-to-all(f32[32,8,128]{2,1,0:T(8,128)S(1)} %broadcast_in_dim.10), channel_id=1, replica_groups=mesh['x'=4,'z'=8,'core'=2,'y'=8] {'x','z'}, dimensions={0} | all-to-all | bytes 262144 | tf_op jit(solution)/shard_map/all_to_all | solution.py:268
  102.5 0.6 slice_bitcast_fusion
  (4 shorter events, 0.1 us)
Async XLA Ops:
  1.7 16.7 %collective-permute-start.1 = (f32[17,4,16,128]{3,2,1,0:T(8,128)S(1)}, f32[17,4,16,128]{3,2,1,0:T(8,128)S(1)}, u32[]{:S(2)}, u32[]{:S(2)}) collective-permute-start(f32[17,4,16,128]{3,2,1,0:T(8,128)S(1)} %pad_maximum_fusion.own.fown), channel_id=1, source_target_pairs={{0,504},{8,16},{16,8},{24,32},{32,24},{40,48},{48,40},{56,64},{64,... | collective-permute-start | bytes 1671176 | tf_op jit(solution)/shard_map/ppermute | solution.py:227
  7.1 12.2 %collective-permute-start = (f32[17,4,16,128]{3,2,1,0:T(8,128)S(1)}, f32[17,4,16,128]{3,2,1,0:T(8,128)S(1)}, u32[]{:S(2)}, u32[]{:S(2)}) collective-permute-start(f32[17,4,16,128]{3,2,1,0:T(8,128)S(1)} %pad_maximum_fusion.own.fown), channel_id=1, source_target_pairs={{0,8},{8,0},{1,9},{9,1},{2,10},{10,2},{3,11},{11,3},{4,12},{12,4},... | collective-permute-start | bytes 1671176 | tf_op jit(solution)/shard_map/ppermute | solution.py:228
  20.6 13.4 %collective-permute-start.3 = (f32[16,4,16,128]{3,2,1,0:T(8,128)S(1)}, f32[16,4,16,128]{3,2,1,0:T(8,128)S(1)}, u32[]{:S(2)}, u32[]{:S(2)}) collective-permute-start(f32[16,4,16,128]{3,2,1,0:T(8,128)S(1)} %get-tuple-element.13.own.gown), channel_id=1, source_target_pairs={{0,504},{8,16},{16,8},{24,32},{32,24},{40,48},{48,40},{56,64},{64,... | collective-permute-start | bytes 1572872 | tf_op jit(solution)/shard_map/ppermute | solution.py:227
  22.5 12.2 %collective-permute-start.2 = (f32[16,4,16,128]{3,2,1,0:T(8,128)S(1)}, f32[16,4,16,128]{3,2,1,0:T(8,128)S(1)}, u32[]{:S(2)}, u32[]{:S(2)}) collective-permute-start(f32[16,4,16,128]{3,2,1,0:T(8,128)S(1)} %get-tuple-element.13.own.gown), channel_id=1, source_target_pairs={{0,8},{8,0},{1,9},{9,1},{2,10},{10,2},{3,11},{11,3},{4,12},{12,4},... | collective-permute-start | bytes 1572872 | tf_op jit(solution)/shard_map/ppermute | solution.py:228
  57.4 8.5 %collective-permute-start.4 = (f32[8,8,8,128]{3,2,1,0:T(8,128)S(1)}, f32[8,8,8,128]{3,2,1,0:T(8,128)S(1)}, u32[]{:S(2)}, u32[]{:S(2)}) collective-permute-start(f32[8,8,8,128]{3,2,1,0:T(8,128)S(1)} %shard_map.54), channel_id=1, source_target_pairs={{0,8},{8,16},{16,24},{24,32},{32,40},{40,48},{48,56},{56,64},{64,7... | collective-permute-start | bytes 786440 | tf_op jit(solution)/shard_map/ppermute | solution.py:249

commit v7 on v6

--- a/solution.py
+++ b/solution.py
@@ -99,8 +99,7 @@
 
 def stage_two(gown, on, off, own_xy, fown, diag, out, send):
     orbs, planes, rows, lanes = gown.shape
-    peers, depth, octet, _ = send.shape
-    chunk = lanes // peers
+    peers, chunk, octet, _ = send.shape
 
     def run(lo, hi):
         def step(group, carry):
@@ -115,9 +114,7 @@
             for i, p in enumerate(octets):
                 lines = jnp.concatenate(us[2 * i : 2 * i + 2], axis=0).T
                 for k in range(peers):
-                    at = (k + 1) % peers * chunk
-                    send[k, :chunk, pl.ds(p, 1), :] = lines[k * chunk : (k + 1) * chunk][:, None, :]
-                    send[k, chunk:, pl.ds(p, 1), :] = lines[at : at + depth - chunk][:, None, :]
+                    send[k, :, pl.ds(p, 1), :] = lines[k * chunk : (k + 1) * chunk][:, None, :]
             return carry
 
         lax.fori_loop(0, 2 * octet // SIDE, step, 0)
@@ -129,7 +126,8 @@
     return lax.broadcasted_iota(jnp.int32, like.shape, 2)
 
 
-def pack_edge(got, out):
+def pack_edge(got, out, head):
+    head[...] = got[:, :2]
     for j in range(out.shape[0]):
         a, b = got[:, 2 * j], got[:, 2 * j + 1]
         out[j] = jnp.where(lane_ids(a) % 64 < 32, pltpu.roll(a, 96, 2), b)
@@ -156,25 +154,29 @@
     return jnp.stack([top, end], axis=1).reshape(-1, a.shape[-1])
 
 
-def gram_own(got, half_diag, u, over, half, first, kept, done):
+def gram_own(got, half_diag, u, over, half, first, last, kept, done):
     keep = pltpu.make_async_copy(u, kept, done)
     keep.start()
     bands, depth, octet, _ = got.shape
-    start = pl.multiple_of(lax.axis_index("y") * (depth - 2), 16)
+    start = pl.multiple_of(lax.axis_index("y") * depth, 16)
     lane = lane_ids(got[:, 0])
     x = lane % 16
     z = lane % 64 // 16
 
     def one_sided(y):
         u = got[:, y]
-        near = got[:, y + 1] + jnp.where(x < 15, pltpu.roll(u, 127, 2), pltpu.roll(u, 15, 2))
-        far = got[:, y + 2] + jnp.where(x < 14, pltpu.roll(u, 126, 2), pltpu.roll(u, 14, 2))
+        near = jnp.where(x < 15, pltpu.roll(u, 127, 2), pltpu.roll(u, 15, 2))
+        far = jnp.where(x < 14, pltpu.roll(u, 126, 2), pltpu.roll(u, 14, 2))
+        if y + 1 < depth:
+            near = near + got[:, y + 1]
+        if y + 2 < depth:
+            far = far + got[:, y + 2]
         near = near + jnp.where(z >= 1, pltpu.roll(u, 16, 2), 0.0)
         far = far + jnp.where(z >= 2, pltpu.roll(u, 32, 2), 0.0)
         return half_diag[pl.ds(start + y, 1), :][None] * u + NEAR * near + FAR * far
 
     total_over, total_half = 0.0, 0.0
-    for y in range(0, depth - 2, 2):
+    for y in range(0, depth, 2):
         u = split(orbital_rows(got[:, y], got[:, y + 1]))
         w = split(orbital_rows(one_sided(y), one_sided(y + 1)))
         total_over = total_over + dot3(u, u)
@@ -186,10 +188,11 @@
         for y in (4 * j, 4 * j + 2):
             two.append(jnp.where(lane % 64 < 32, got[:, y], pltpu.roll(got[:, y + 1], 32, 2)))
         first[j] = orbital_rows(*two)
+    last[...] = orbital_rows(got[:, depth - 2], got[:, depth - 1])
     keep.wait()
 
 
-def gram_edge(edge, first, over, half, out):
+def gram_edge(edge, head, first, last, over, half, out):
     bands = edge.shape[1]
     third = lane_ids(edge[0]) % 32 < 16
     total = half[...]
@@ -198,6 +201,8 @@
         for e in (edge[2 * j], edge[2 * j + 1]):
             two.append(FAR * e + jnp.where(third, NEAR * pltpu.roll(e, 112, 2), 0.0))
         total = total + dot3(split(first[j]), split(orbital_rows(*two)))
+    one, two = head[:, 0], head[:, 1]
+    total = total + dot3(split(last[...]), split(orbital_rows(FAR * one, NEAR * one + FAR * two)))
     out[:, 0] = over[...].reshape(bands, -1, total.shape[-1])
     out[:, 1] = (total + total.T).reshape(bands, -1, total.shape[-1])
 
@@ -236,7 +241,7 @@
     total = bands * orbs
     u, send = call(
         stage_two,
-        [orbitals.shape, (bands, lanes // bands + 2, orbs // 2, 2 * planes * rows)],
+        [orbitals.shape, (bands, lanes // bands, orbs // 2, 2 * planes * rows)],
         g,
         on,
         off,
@@ -245,12 +250,14 @@
         diag,
     )
     got = lax.all_to_all(send, "y", 0, 0, tiled=True)
-    (edge,) = call(pack_edge, [(lanes // bands // 2, bands, orbs // 2, 2 * planes * rows)], got)
+    tile = (bands, orbs // 2, 2 * planes * rows)
+    edge, head = call(pack_edge, [(lanes // bands // 2, *tile), (bands, 2, *tile[1:])], got)
     edge = lax.ppermute(edge, GRID, following)
+    head = lax.ppermute(head, "y", ring_shift(bands, -1))
     firsts = (lanes // bands // 4, total, 2 * planes * rows)
-    over, half, first, u = call(
+    over, half, first, last, u = call(
         gram_own,
-        [(total, total), (total, total), firsts, u.shape],
+        [(total, total), (total, total), firsts, firsts[1:], u.shape],
         got,
         half_diag,
         u,
@@ -258,7 +265,7 @@
         scratch=[pltpu.SemaphoreType.DMA],
         flops=1 << 30,
     )
-    (part,) = call(gram_edge, [(bands, 2, orbs, total)], edge, first, over, half)
+    (part,) = call(gram_edge, [(bands, 2, orbs, total)], edge, head, first, last, over, half)
 
     pieces = lax.axis_size(REDUCERS)
     flat = part.reshape(pieces, -1, bands * orbs)

time: 104 us -> 103 us (level)
  waiting for transfers between devices: 6.13 us -> 4.07 us
  starting transfers between devices: 30.5 us -> 32.4 us
    ppermute x1, waiting for transfers between devices: 4.56 us -> 1.45 us  [per_device(): edge = lax.ppermute(edge, GRID, following)]
    ppermute x0 -> x1, starting transfers between devices: none -> 1.92 us  [per_device(): head = lax.ppermute(head, 'y', ring_shift(bands, -1))]
    all_to_all x1, blocking collectives: 20.9 us -> 19.6 us  [per_device(): got = lax.all_to_all(send, 'y', 0, 0, tiled=True)]
    ppermute x0 -> x1, waiting for transfers between devices: none -> 1.04 us  [per_device(): head = lax.ppermute(head, 'y', ring_shift(bands, -1))]
  transfers between devices with their start and end apart: 5 -> 6, of which waited for: 3 -> 4; matrix products, arithmetic and copies ran while one was open for 0% -> 0% of each run, Pallas kernels for 3% -> 3%
where the time goes in v7:
time: 103 us; the launch traced here: 102 us
  blocking collectives  55.9 us (54%)
  starting transfers between devices  32.4 us (31%)
  Pallas kernels  7.23 us (7%)
  waiting for transfers between devices  4.07 us (4%)
  other arithmetic  1.16 us (1%)
    ppermute x2, starting transfers between devices, both_sides(): return (lax.ppermute(slab, 'core', [(0, 1), (1, 0)]), off)  21.3 us
    all_to_all x1, blocking collectives, per_device(): got = lax.all_to_all(send, 'y', 0, 0, tiled=True)  19.6 us
    all_to_all x1, blocking collectives, per_device(): back = lax.all_to_all(spread, ('x', 'z'), 0, 0, tiled=True)  12.5 us
    all_to_all x1, blocking collectives, per_device(): mine = lax.all_to_all(flat, REDUCERS, 0, 0, tiled=True).sum(0)  12.5 us
    psum x1, blocking collectives, per_device(): mine = lax.psum(mine, 'core')  11.3 us
    ppermute x2, starting transfers between devices, both_sides(): off = lax.ppermute(slab, GRID, outer)  7.31 us
    pallas_call x7, Pallas kernels, call(): pl.pallas_call(body, out_shape=[jax.ShapeDtypeStruct(s, jnp.float32) for...  7.23 us
  transfers between devices with their start and end apart: 6, of which 4 were waited for; matrix products, arithmetic and copies ran while one was open for 0% of the time, Pallas kernels for 3%

profile of v7, /device:TPU:1, one launch (start us, length us, event | category | flops | bytes accessed | tf_op | source)
XLA Modules:
  0.0 102.2 jit_solution(10719450304282653598)
XLA Ops:
  0.6 1.1 %pad_maximum_fusion.own.fown = f32[17,4,16,128]{3,2,1,0:T(8,128)S(1)} fusion(f32[1,4,16,128]{3,2,1,0:T(8,128)} %bitcast.9, f32[16,4,16,128]{3,2,1,0:T(8,128)} %param.2), kind=kLoop, calls=%fused_computation | loop fusion | flops 139264 | bytes 1114112 | tf_op jit(solution)/shard_map/concatenate | solution.py:235
  1.7 5.4 %collective-permute-start.1 = (f32[17,4,16,128]{3,2,1,0:T(8,128)S(1)}, f32[17,4,16,128]{3,2,1,0:T(8,128)S(1)}, u32[]{:S(2)}, u32[]{:S(2)}) collective-permute-start(f32[17,4,16,128]{3,2,1,0:T(8,128)S(1)} %pad_maximum_fusion.own.fown), channel_id=1, source_target_pairs={{0,504},{8,16},{16,8},{24,32},{32,24},{40,48},{48,40},{56,64},{64,... | collective-permute-start | bytes 1671176 | tf_op jit(solution)/shard_map/ppermute | solution.py:232
  7.1 10.6 %collective-permute-start = (f32[17,4,16,128]{3,2,1,0:T(8,128)S(1)}, f32[17,4,16,128]{3,2,1,0:T(8,128)S(1)}, u32[]{:S(2)}, u32[]{:S(2)}) collective-permute-start(f32[17,4,16,128]{3,2,1,0:T(8,128)S(1)} %pad_maximum_fusion.own.fown), channel_id=1, source_target_pairs={{0,8},{8,0},{1,9},{9,1},{2,10},{10,2},{3,11},{11,3},{4,12},{12,4},... | collective-permute-start | bytes 1671176 | tf_op jit(solution)/shard_map/ppermute | solution.py:233
  17.8 0.7 shard_map.49.own_xy
  18.4 0.0 collective-permute-done.1.off
  18.5 0.9 collective-permute-done.on
  19.3 1.3 %shard_map.50 = (f32[16,4,16,128]{3,2,1,0:T(8,128)S(1)}, f32[8,16,128]{2,1,0:T(8,128)S(1)}) custom-call(f32[17,4,16,128]{3,2,1,0:T(8,128)S(1)} %pad_maximum_fusion.own.fown, f32[17,4,16,128]{3,2,1,0:T(8,128)S(1)} %collective-permute-done.on, f32[17,4,16,128]{3,2,1,0:T(8,128)S(1)} %collective-permute-done.1.off, f32[16,4,16,128]{3,2,1,0:T(8,128)S(1)} %shard_map.49.own_xy), custom_call_target="tpu_custom_call" | custom-call | bytes 1048576 | tf_op jit(solution)/shard_map/pallas_call | solution.py:212
  20.6 1.9 %collective-permute-start.3 = (f32[16,4,16,128]{3,2,1,0:T(8,128)S(1)}, f32[16,4,16,128]{3,2,1,0:T(8,128)S(1)}, u32[]{:S(2)}, u32[]{:S(2)}) collective-permute-start(f32[16,4,16,128]{3,2,1,0:T(8,128)S(1)} %get-tuple-element.16.own.gown), channel_id=1, source_target_pairs={{0,504},{8,16},{16,8},{24,32},{32,24},{40,48},{48,40},{56,64},{64,... | collective-permute-start | bytes 1572872 | tf_op jit(solution)/shard_map/ppermute | solution.py:232
  22.5 10.7 %collective-permute-start.2 = (f32[16,4,16,128]{3,2,1,0:T(8,128)S(1)}, f32[16,4,16,128]{3,2,1,0:T(8,128)S(1)}, u32[]{:S(2)}, u32[]{:S(2)}) collective-permute-start(f32[16,4,16,128]{3,2,1,0:T(8,128)S(1)} %get-tuple-element.16.own.gown), channel_id=1, source_target_pairs={{0,8},{8,0},{1,9},{9,1},{2,10},{10,2},{3,11},{11,3},{4,12},{12,4},... | collective-permute-start | bytes 1572872 | tf_op jit(solution)/shard_map/ppermute | solution.py:233
  33.2 0.8 shard_map.51
  34.0 0.0 collective-permute-done.3.off
  34.0 0.7 collective-permute-done.2.on
  34.7 1.6 %shard_map.52 = (f32[16,4,16,128]{3,2,1,0:T(8,128)S(1)}, f32[8,16,8,128]{3,2,1,0:T(8,128)S(1)}) custom-call(f32[16,4,16,128]{3,2,1,0:T(8,128)S(1)} %get-tuple-element.16.own.gown, f32[16,4,16,128]{3,2,1,0:T(8,128)S(1)} %collective-permute-done.2.on, f32[16,4,16,128]{3,2,1,0:T(8,128)S(1)} %collective-permute-done.3.off, ...), custom_call_target="tpu_custom_call" | custom-call | bytes 1048576 | tf_op jit(solution)/shard_map/pallas_call | solution.py:212
  36.3 19.6 %all_to_all.15.got = f32[8,16,8,128]{3,2,1,0:T(8,128)S(1)} all-to-all(f32[8,16,8,128]{3,2,1,0:T(8,128)S(1)} %get-tuple-element.19), channel_id=1, replica_groups=mesh['x'=4,'z'=8,'core'=2,'y'=8] {'y'}, dimensions={0} | all-to-all | bytes 1048576 | tf_op jit(solution)/shard_map/all_to_all | solution.py:252
  55.9 0.1 shard_map.54
  56.0 1.9 %collective-permute-start.4 = (f32[8,8,8,128]{3,2,1,0:T(8,128)S(1)}, f32[8,8,8,128]{3,2,1,0:T(8,128)S(1)}, u32[]{:S(2)}, u32[]{:S(2)}) collective-permute-start(f32[8,8,8,128]{3,2,1,0:T(8,128)S(1)} %get-tuple-element.23), channel_id=1, source_target_pairs={{0,8},{8,16},{16,24},{24,32},{32,40},{40,48},{48,56},{56,64},{64,7... | collective-permute-start | bytes 786440 | tf_op jit(solution)/shard_map/ppermute | solution.py:255
  58.0 1.9 %collective-permute-start.5 = (f32[8,2,8,128]{3,2,1,0:T(8,128)S(1)}, f32[8,2,8,128]{3,2,1,0:T(8,128)S(1)}, u32[]{:S(2)}, u32[]{:S(2)}) collective-permute-start(f32[8,2,8,128]{3,2,1,0:T(8,128)S(1)} %get-tuple-element.24), channel_id=1, source_target_pairs={{0,7},{1,0},{2,1},{3,2},{4,3},{5,4},{6,5},{7,6},{8,15},{9,8},{10,9... | collective-permute-start | bytes 196616 | tf_op jit(solution)/shard_map/ppermute | solution.py:256
  59.9 2.0 %shard_map.53 = (f32[128,128]{1,0:T(8,128)S(1)}, f32[128,128]{1,0:T(8,128)S(1)}, f32[4,128,128]{2,1,0:T(8,128)S(1)}, f32[128,128]{1,0:T(8,128)S(1)}, f32[16,4,16,128]{3,2,1,0:T(8,128)}) custom-call(f32[8,16,8,128]{3,2,1,0:T(8,128)S(1)} %all_to_all.15.got, f32[128,128]{1,0:T(8,128)S(1)} %get-tuple-element.20.half_diag, f32[16,4,16,128]{3,2,1,0:T(8,128)S(1)} %get-tuple-element.21.u), custom_call_target="tpu_custom_call" | custom-call | flops 1073741824 | bytes 1048576 | tf_op jit(solution)/shard_map/pallas_call | solution.py:212
  61.9 1.0 %collective-permute-done.5.head = f32[8,2,8,128]{3,2,1,0:T(8,128)S(1)} collective-permute-done((f32[8,2,8,128]{3,2,1,0:T(8,128)S(1)}, f32[8,2,8,128]{3,2,1,0:T(8,128)S(1)}, u32[]{:S(2)}, u32[]{:S(2)}) %collective-permute-start.5) | collective-permute-done | bytes 65568 | tf_op jit(solution)/shard_map/ppermute | solution.py:256
  63.0 1.5 %collective-permute-done.4.edge = f32[8,8,8,128]{3,2,1,0:T(8,128)S(1)} collective-permute-done((f32[8,8,8,128]{3,2,1,0:T(8,128)S(1)}, f32[8,8,8,128]{3,2,1,0:T(8,128)S(1)}, u32[]{:S(2)}, u32[]{:S(2)}) %collective-permute-start.4) | collective-permute-done | bytes 262176 | tf_op jit(solution)/shard_map/ppermute | solution.py:255
  64.4 0.8 shard_map.55
  65.2 12.5 %all_to_all.16 = f32[32,8,128]{2,1,0:T(8,128)S(1)} all-to-all(f32[32,8,128]{2,1,0:T(8,128)S(1)} %bitcast.8), channel_id=1, replica_groups=mesh['x'=4,'z'=8,'core'=2,'y'=8] {'y','x'}, dimensions={0} | all-to-all | bytes 262144 | tf_op jit(solution)/shard_map/all_to_all | solution.py:272
  77.7 11.3 %psum.7 = f32[8,128]{1,0:T(8,128)S(1)} all-reduce(f32[8,128]{1,0:T(8,128)S(1)} %reduce_sum.18), channel_id=1, replica_groups=mesh['x'=4,'z'=8,'core'=2,'y'=8] {'core'}, use_global_device_ids=true, to_apply=%region_1.0 | all-reduce | flops 1024 | bytes 8192 | tf_op jit(solution)/shard_map/psum | solution.py:273
  89.0 12.5 %all_to_all.17 = f32[32,8,128]{2,1,0:T(8,128)S(1)} all-to-all(f32[32,8,128]{2,1,0:T(8,128)S(1)} %broadcast_in_dim.10), channel_id=1, replica_groups=mesh['x'=4,'z'=8,'core'=2,'y'=8] {'x','z'}, dimensions={0} | all-to-all | bytes 262144 | tf_op jit(solution)/shard_map/all_to_all | solution.py:275
  101.6 0.6 slice_bitcast_fusion
  (4 shorter events, 0.1 us)
Async XLA Ops:
  1.7 16.7 %collective-permute-start.1 = (f32[17,4,16,128]{3,2,1,0:T(8,128)S(1)}, f32[17,4,16,128]{3,2,1,0:T(8,128)S(1)}, u32[]{:S(2)}, u32[]{:S(2)}) collective-permute-start(f32[17,4,16,128]{3,2,1,0:T(8,128)S(1)} %pad_maximum_fusion.own.fown), channel_id=1, source_target_pairs={{0,504},{8,16},{16,8},{24,32},{32,24},{40,48},{48,40},{56,64},{64,... | collective-permute-start | bytes 1671176 | tf_op jit(solution)/shard_map/ppermute | solution.py:232
  7.1 12.2 %collective-permute-start = (f32[17,4,16,128]{3,2,1,0:T(8,128)S(1)}, f32[17,4,16,128]{3,2,1,0:T(8,128)S(1)}, u32[]{:S(2)}, u32[]{:S(2)}) collective-permute-start(f32[17,4,16,128]{3,2,1,0:T(8,128)S(1)} %pad_maximum_fusion.own.fown), channel_id=1, source_target_pairs={{0,8},{8,0},{1,9},{9,1},{2,10},{10,2},{3,11},{11,3},{4,12},{12,4},... | collective-permute-start | bytes 1671176 | tf_op jit(solution)/shard_map/ppermute | solution.py:233
  20.6 13.4 %collective-permute-start.3 = (f32[16,4,16,128]{3,2,1,0:T(8,128)S(1)}, f32[16,4,16,128]{3,2,1,0:T(8,128)S(1)}, u32[]{:S(2)}, u32[]{:S(2)}) collective-permute-start(f32[16,4,16,128]{3,2,1,0:T(8,128)S(1)} %get-tuple-element.16.own.gown), channel_id=1, source_target_pairs={{0,504},{8,16},{16,8},{24,32},{32,24},{40,48},{48,40},{56,64},{64,... | collective-permute-start | bytes 1572872 | tf_op jit(solution)/shard_map/ppermute | solution.py:232
  22.5 12.2 %collective-permute-start.2 = (f32[16,4,16,128]{3,2,1,0:T(8,128)S(1)}, f32[16,4,16,128]{3,2,1,0:T(8,128)S(1)}, u32[]{:S(2)}, u32[]{:S(2)}) collective-permute-start(f32[16,4,16,128]{3,2,1,0:T(8,128)S(1)} %get-tuple-element.16.own.gown), channel_id=1, source_target_pairs={{0,8},{8,0},{1,9},{9,1},{2,10},{10,2},{3,11},{11,3},{4,12},{12,4},... | collective-permute-start | bytes 1572872 | tf_op jit(solution)/shard_map/ppermute | solution.py:233
  56.0 8.4 %collective-permute-start.4 = (f32[8,8,8,128]{3,2,1,0:T(8,128)S(1)}, f32[8,8,8,128]{3,2,1,0:T(8,128)S(1)}, u32[]{:S(2)}, u32[]{:S(2)}) collective-permute-start(f32[8,8,8,128]{3,2,1,0:T(8,128)S(1)} %get-tuple-element.23), channel_id=1, source_target_pairs={{0,8},{8,16},{16,24},{24,32},{32,40},{40,48},{48,56},{56,64},{64,7... | collective-permute-start | bytes 786440 | tf_op jit(solution)/shard_map/ppermute | solution.py:255
  58.0 5.0 %collective-permute-start.5 = (f32[8,2,8,128]{3,2,1,0:T(8,128)S(1)}, f32[8,2,8,128]{3,2,1,0:T(8,128)S(1)}, u32[]{:S(2)}, u32[]{:S(2)}) collective-permute-start(f32[8,2,8,128]{3,2,1,0:T(8,128)S(1)} %get-tuple-element.24), channel_id=1, source_target_pairs={{0,7},{1,0},{2,1},{3,2},{4,3},{5,4},{6,5},{7,6},{8,15},{9,8},{10,9... | collective-permute-start | bytes 196616 | tf_op jit(solution)/shard_map/ppermute | solution.py:256
